TPU v7x, 512 devices: a whole 4x8x8 slice. The times are simulated.
512 devices in a mesh: roll: 64 (over y_hi, z, core), tp: 8 (over x, y_lo).
Axes of the slice: x: 4, y: 8 (y_hi: 4, y_lo: 2; y = y_hi * 2 + y_lo), z: 8, core: 2. Of those that a mesh axis runs over, the one named last changes fastest.
Arguments:
- hidden: bfloat16 [4, 4096, 5120], P(None, ('roll', 'tp')), may hold values from -6 to 6
- queries: bfloat16 [4, 4096, 4096], P(None, 'roll', 'tp'), may hold values from -6 to 6
- key_cache: bfloat16 [4096, 32, 1024], P('roll', None, 'tp'), may hold values from -6 to 6
- value_cache: bfloat16 [4096, 32, 1024], P('roll', None, 'tp'), may hold values from -6 to 6
- cache_len: int32 [4096], P('roll'), may hold values from 2 to 32, as said below
- base_key: bfloat16 [5120, 1024], P(None, 'tp'), may hold values from -0.078125 to 0.078125
- base_value: bfloat16 [5120, 1024], P(None, 'tp'), may hold values from -0.078125 to 0.078125
- factor_a: bfloat16 [64, 2, 5120, 64], P('roll', None, 'tp'), may hold values from -0.078125 to 0.078125
- factor_b: bfloat16 [64, 2, 64, 1024], P('roll', None, None, 'tp'), may hold values from -0.375 to 0.375
- owner: int32 [2], replicated, may hold values from 0 to 63
Outputs:
- attended: bfloat16 [4, 4096, 4096], P(None, 'roll', 'tp')
Inputs may be any that keep to these rules, and one draw needn't show every extreme that they name: `cache_len`: the first sample of each rollout group uses all 32 positions.
All inputs are finite; a program needn't handle non-finite values.
Results may differ from a plain program's by a relative error of at most 0.008.
Values may be sent and summed in bfloat16 or wider, within the bound.
A program may use at most 64 MiB of HBM per device.

v0:
```python
import math

import jax
import jax.numpy as jnp
from jax import lax
from jax.sharding import PartitionSpec as P

D = 5120
KVH = 8
HD = 128
QPK = 4
STEPS = 4


def broadcast(value, axis, source):
    kept = jnp.where(lax.axis_index(axis) == source, value, 0).astype(value.dtype)
    return lax.psum(kept, axis)


def local(
    hidden,
    queries,
    key_cache,
    value_cache,
    cache_len,
    base_key,
    base_value,
    factor_a,
    factor_b,
    owner,
):
    current = []
    for member in range(2):
        current.append(
            (
                broadcast(factor_a[0, member], "roll", owner[member]),
                broadcast(factor_b[0, member], "roll", owner[member]),
            )
        )
    down_rows = (
        lax.all_gather(current[0][0], "tp", axis=0, tiled=True),
        lax.all_gather(current[1][0], "tp", axis=0, tiled=True),
    )
    heads_here = KVH // lax.axis_size("tp")
    merged = []
    for member, weights in ((0, base_key), (1, base_value)):
        update = jnp.dot(down_rows[member], current[member][1], preferred_element_type=jnp.float32)
        merged.append(
            (weights.astype(jnp.float32) + update)
            .astype(jnp.bfloat16)
            .reshape(D, heads_here, 1, HD)
        )
    both_weights = jnp.concatenate(merged, axis=2).reshape(D, heads_here, 2 * HD)
    projected = jnp.einsum(
        "trd,dhc->trhc",
        lax.all_gather(hidden, "tp", axis=1, tiled=True),
        both_weights,
        preferred_element_type=jnp.float32,
    )
    fresh = projected.astype(jnp.bfloat16)
    samples_here = fresh.shape[1]
    new_key = fresh[..., :HD]
    new_value = fresh[..., HD:].astype(jnp.float32)
    positions = key_cache.shape[1]
    query_heads = queries.reshape(STEPS, samples_here, heads_here, QPK, HD)
    cached_keys = key_cache.reshape(samples_here, positions, heads_here, HD)
    cached_values = value_cache.reshape(samples_here, positions, heads_here, HD).astype(jnp.float32)
    scale = 1.0 / math.sqrt(HD)
    cache_scores = (
        jnp.einsum(
            "tshjd,schd->tshjc", query_heads, cached_keys, preferred_element_type=jnp.float32
        )
        * scale
    )
    new_scores = (
        jnp.einsum("tshjd,ushd->tshju", query_heads, new_key, preferred_element_type=jnp.float32)
        * scale
    )
    cache_mask = (jnp.arange(positions)[None, :] < cache_len[:, None])[None, :, None, None, :]
    new_mask = (jnp.arange(STEPS)[None, :] <= jnp.arange(STEPS)[:, None])[:, None, None, None, :]
    top = jnp.maximum(
        jnp.max(jnp.where(cache_mask, cache_scores, -jnp.inf), axis=-1),
        jnp.max(jnp.where(new_mask, new_scores, -jnp.inf), axis=-1),
    )
    cache_weight = jnp.where(cache_mask, jnp.exp(cache_scores - top[..., None]), 0.0)
    new_weight = jnp.where(new_mask, jnp.exp(new_scores - top[..., None]), 0.0)
    total = jnp.sum(cache_weight, axis=-1) + jnp.sum(new_weight, axis=-1)
    summed_values = jnp.einsum("tshjc,schd->tshjd", cache_weight, cached_values) + jnp.einsum(
        "tshju,ushd->tshjd", new_weight, new_value
    )
    attended = summed_values / total[..., None]
    return attended.reshape(STEPS, samples_here, heads_here * QPK * HD).astype(jnp.bfloat16)


def solution(mesh):
    placed = (
        P(None, ("roll", "tp"), None),
        P(None, "roll", "tp"),
        P("roll", None, "tp"),
        P("roll", None, "tp"),
        P("roll"),
        P(None, "tp"),
        P(None, "tp"),
        P("roll", None, "tp", None),
        P("roll", None, None, "tp"),
        P(),
    )
    return jax.shard_map(
        local, mesh=mesh, in_specs=placed, out_specs=P(None, "roll", "tp"), check_vma=False
    )
```

profile of v0, /device:TPU:1, one launch (start us, length us, event | category | flops | bytes accessed | tf_op | source)
XLA Modules:
  0.0 599.3 jit_solution(17319054662946514156)
XLA Ops:
  7.4 0.0 copy-start
  7.4 0.0 all-reduce.4.cloned.1.call-start
  7.4 1.3 fusion.28
  10.0 1.6 select_bitcast_fusion.1
  11.6 0.0 all-reduce.4.cloned.1.call-update
  11.6 0.0 all-gather.2.cloned.1.call-start
  11.7 0.5 all-gather.2.cloned.1.call-update
  12.2 0.0 copy-start.2
  12.2 0.0 copy-start.5
  12.2 0.0 copy-start.6
  12.2 1.6 copy.13
  13.9 1.6 copy.12
  15.5 0.0 copy-done.2
  15.5 0.8 reshape.126
  16.3 0.0 copy-done.5
  16.3 283.2 %all-reduce = (bf16[64,128]{1,0:T(8,128)(2,1)S(1)}, bf16[64,128]{1,0:T(8,128)(2,1)S(1)}) all-reduce(bf16[64,128]{1,0:T(8,128)(2,1)S(1)} %get-tuple-element.14, bf16[64,128]{1,0:T(8,128)(2,1)S(1)} %get-tuple-element.13), channel_id=1, replica_groups=mesh['roll'=64,'tp'=8] {'roll'}, use_global_device_ids=true, to_apply=%region_4.5 | all-reduce | flops 16384 | bytes 65536 | tf_op jit(solution)/shard_map/psum | solution.py:17
  299.4 0.0 copy-done.6
  299.4 0.1 iota_compare_fusion
  299.5 2.4 select_reduce_fusion.1
  301.9 229.9 %all-reduce.4.cloned.1.call-done = (bf16[640,64]{0,1:T(8,128)(2,1)}, bf16[640,64]{0,1:T(8,128)(2,1)}) async-done(((bf16[640,64]{0,1:T(8,128)(2,1)}, bf16[640,64]{0,1:T(8,128)(2,1)}), (bf16[640,64]{0,1:T(8,128)(2,1)}, bf16[640,64]{0,1:T(8,128)(2,1)})) %all-reduce.4.cloned.1.call-update) | async-done | bytes 163856 | tf_op jit(solution)/shard_map/psum | solution.py:17
  531.8 0.0 copy-start.4
  531.8 25.7 %all_gather.10 = bf16[5120,64]{0,1:T(8,128)(2,1)S(1)} all-gather(bf16[640,64]{0,1:T(8,128)(2,1)} %get-tuple-element.7), channel_id=1, replica_groups=mesh['roll'=64,'tp'=8] {'tp'}, dimensions={0}, use_global_device_ids=true | all-gather | bytes 737280 | tf_op jit(solution)/shard_map/all_gather | solution.py:42
  557.5 0.6 fusion.2
  558.1 0.0 copy-done.4
  558.1 24.3 %all_gather.9 = bf16[5120,64]{0,1:T(8,128)(2,1)S(1)} all-gather(bf16[640,64]{0,1:T(8,128)(2,1)S(1)} %copy-done.4), channel_id=1, replica_groups=mesh['roll'=64,'tp'=8] {'tp'}, dimensions={0}, use_global_device_ids=true | all-gather | bytes 737280 | tf_op jit(solution)/shard_map/all_gather | solution.py:41
  582.4 0.5 fusion.3
  582.9 0.2 pad_maximum_fusion
  583.2 0.0 all-gather.2.cloned.1.call-done
  583.2 0.0 copy-start.3
  583.2 2.7 fusion.7
  585.9 0.0 copy-start.1
  586.0 0.0 copy-done.3
  586.0 2.4 select_reduce_fusion
  588.4 0.5 fusion.15
  589.0 0.0 copy-done.1
  589.0 0.8 fusion.14
  589.8 0.0 copy-done
  589.8 0.6 convolution_bitcast_fusion
  590.4 0.7 fusion.9
  591.0 0.1 convert_element_type.43
  591.2 0.7 copy.19
  (5 shorter events, 0.1 us)
Async XLA Ops:
  7.4 582.4 %copy-start = (bf16[64,32,128]{2,1,0:T(8,128)(2,1)S(1)}, bf16[64,32,128]{2,1,0:T(8,128)(2,1)}, u32[]{:S(2)}) copy-start(bf16[64,32,128]{2,1,0:T(8,128)(2,1)} %param.13) | copy-start | bytes 1572868
  7.4 524.4 %all-reduce.4.cloned.1.call-start = ((), (), s32[]{:S(2)}) async-start(), calls=%async_computation.1 | async-start | bytes 327680 | tf_op jit(solution)/shard_map/psum | solution.py:17
  11.6 571.6 %all-gather.2.cloned.1.call-start = ((), (), s32[]{:S(2)}) async-start(), calls=%async_computation | async-start | bytes 2949120 | tf_op jit(solution)/shard_map/all_gather | solution.py:56
  12.2 3.3 copy-start.2
  12.2 4.1 copy-start.5
  12.2 287.2 %copy-start.6 = (s32[64]{0:T(128)S(1)}, s32[64]{0:T(128)}, u32[]{:S(2)}) copy-start(s32[64]{0:T(128)} %param.14) | copy-start | bytes 772
  531.8 26.3 %copy-start.4 = (bf16[640,64]{0,1:T(8,128)(2,1)S(1)}, bf16[640,64]{0,1:T(8,128)(2,1)}, u32[]{:S(2)}) copy-start(bf16[640,64]{0,1:T(8,128)(2,1)} %get-tuple-element.8) | copy-start | bytes 245764
  583.2 2.7 copy-start.3
  585.9 3.1 copy-start.1
Sparse Core Ops, SparseCore 0:
  11.7 520.0 all-reduce.3
Sparse Core Ops, SparseCore 1:
  14.4 73.2 all-gather.1
where the time goes:
time: 611 us; the launch traced here: 599 us
  blocking collectives  333 us (55%)
  waiting for transfers between devices  230 us (38%)
  between operations  16.3 us (3%)
  matrix products  9.79 us (2%)
  local copies, waits for them, and re-layouts  6.24 us (1%)
    psum x1, blocking collectives, broadcast(): return lax.psum(kept, axis)  283 us
    psum x1, waiting for transfers between devices, broadcast(): return lax.psum(kept, axis)  230 us
    all_gather x1, blocking collectives, local(): lax.all_gather(current[1][0], 'tp', axis=0, tiled=True)  25.7 us
    all_gather x1, blocking collectives, local(): lax.all_gather(current[0][0], 'tp', axis=0, tiled=True)  24.3 us
  transfers between devices with their start and end apart: 2, of which 1 were waited for; matrix products, arithmetic and copies ran while one was open for 1% of the time, Pallas kernels for 0%

commit v1 on v0

v1 whole, which is shorter than its diff:
```python
import functools
import math

import jax
import jax.numpy as jnp
from jax import lax
from jax.experimental import pallas as pl
from jax.experimental.pallas import tpu as pltpu
from jax.sharding import PartitionSpec as P

D = 5120
HD = 128
QPK = 4
R = 64
STEPS = 4
SAMP = 64
CACHE = 32
TP = 8
CHUNK = D // TP
NC = D // CHUNK
TOK = STEPS * SAMP // TP
CHIPS = 32
PIECES = 24
LANES = (CHUNK + HD) // 128
GROUP = 16
GROUPS = SAMP // GROUP
ROWS = STEPS * QPK * GROUP
NEG = -1e30
MESH = pl.DeviceIdType.MESH
NT = (((1,), (1,)), ((), ()))


def kernel(
    owner, lens, hidden, queries, keys, values, base_key, base_value, down, up, out,
    gathered, weights, kbuf, vbuf, half, other, bins, full, acc, top_ref, sum_ref,
    low_part, low_bins, low_all,
    load_sem, p0_send, p0_recv, p1_send, p1_recv, p2_send, p2_recv, p3_send, p3_recv,
    h_send, h_recv, l_send, l_recv, g_send, g_recv,
):
    roll, tp = lax.axis_index("roll"), lax.axis_index("tp")
    chip, core = roll // 2, roll % 2
    x, y = tp // 2, tp % 2
    pos = lambda px, py: lax.rem(px + 8, 4) * 2 + py
    right, left, across = pos(x + 1, y), pos(x - 1, y), pos(x, 1 - y)

    def remote(src, dst, send, recv, to_roll, to_tp):
        return pltpu.make_async_remote_copy(
            src_ref=src, dst_ref=dst, send_sem=send, recv_sem=recv,
            device_id=(to_roll, to_tp), device_id_type=MESH,
        )

    loads = [
        pltpu.make_async_copy(base_key, weights.at[:, pl.ds(0, HD)], load_sem.at[0]),
        pltpu.make_async_copy(base_value, weights.at[:, pl.ds(HD, HD)], load_sem.at[1]),
        pltpu.make_async_copy(keys, kbuf, load_sem.at[2]),
        pltpu.make_async_copy(values, vbuf, load_sem.at[3]),
    ]
    for c in range(NC):
        loads.append(
            pltpu.make_async_copy(
                hidden.at[:, pl.ds(c * CHUNK, CHUNK)], gathered.at[c, tp], load_sem.at[4 + c]
            )
        )
    for copy in loads:
        copy.start()

    barrier = pltpu.get_barrier_semaphore()

    def greet_tp(d, _):
        pl.semaphore_signal(barrier, inc=1, device_id=(roll, lax.rem(tp + d, TP)), device_id_type=MESH)
        return 0

    def greet_roll(d, _):
        to = lax.rem(chip + d, CHIPS) * 2 + core
        pl.semaphore_signal(barrier, inc=1, device_id=(to, tp), device_id_type=MESH)
        return 0

    pl.semaphore_signal(barrier, inc=1, device_id=(chip * 2 + 1 - core, tp), device_id_type=MESH)
    lax.fori_loop(1, TP, greet_tp, 0)
    lax.fori_loop(1, CHIPS, greet_roll, 0)
    pl.semaphore_wait(barrier, 1 + TP - 1 + CHIPS - 1)

    twin = chip * 2 + 1 - core
    mine = pl.ds(pl.multiple_of(core * R, R), R)
    theirs = pl.ds(pl.multiple_of((1 - core) * R, R), R)
    p0 = [
        remote(down.at[theirs], other.at[:, pl.ds(0, CHUNK)], p0_send.at[0], p0_recv.at[0], twin, tp),
        remote(up.at[theirs], other.at[:, pl.ds(CHUNK, HD)], p0_send.at[1], p0_recv.at[1], twin, tp),
    ]
    for copy in p0:
        copy.start()

    def hop(c, kind, block, to, src=None, rows=None):
        dst = gathered.at[c, block]
        if rows is not None:
            dst = dst.at[rows]
        return remote(dst if src is None else src, dst, h_send.at[c, kind], h_recv.at[c, kind], roll, to)

    sends = []

    def start(copy):
        copy.start()
        sends.append(copy)

    for c in range(NC):
        own = hidden.at[:, pl.ds(c * CHUNK, CHUNK)]
        start(hop(c, 0, tp, across, own))
        start(hop(c, 1, tp, right, own))
        start(hop(c, 2, tp, left, own))

    def landed(c, kind, block, rows=None):
        hop(c, kind, block, across, rows=rows).wait_recv()

    top_rows, low_rows = pl.ds(0, TOK // 2), pl.ds(TOK // 2, TOK // 2)
    far, far_across = pos(x + 2, y), pos(x + 2, 1 - y)

    def spread(c):
        landed(c, 0, across)
        start(hop(c, 3, across, right))
        start(hop(c, 4, across, left))
        landed(c, 1, left)
        start(hop(c, 5, left, right, rows=top_rows))
        landed(c, 2, right)
        start(hop(c, 6, right, left, rows=low_rows))

    def spread_again(c):
        landed(c, 3, pos(x - 1, 1 - y))
        start(hop(c, 7, pos(x - 1, 1 - y), right, rows=top_rows))
        landed(c, 4, pos(x + 1, 1 - y))
        start(hop(c, 8, pos(x + 1, 1 - y), left, rows=low_rows))

    def complete(c):
        landed(c, 5, far, top_rows)
        landed(c, 6, far, low_rows)
        landed(c, 7, far_across, top_rows)
        landed(c, 8, far_across, low_rows)
        loads[4 + c].wait()

    scale = 1.0 / math.sqrt(HD)
    row = lax.broadcasted_iota(jnp.int32, (QPK * GROUP, GROUP * CACHE), 0)
    col = lax.broadcasted_iota(jnp.int32, (QPK * GROUP, GROUP * CACHE), 1)
    same = (row % GROUP) == (col // CACHE)
    col_row = lax.broadcasted_iota(jnp.int32, (1, GROUP * CACHE), 1)

    def block_queries(g, t):
        at = pl.ds(pl.multiple_of(g * GROUP, GROUP), GROUP)
        return jnp.concatenate([queries[t, at, j * HD : (j + 1) * HD] for j in range(QPK)], axis=0)

    def cached(g, _):
        at = pl.ds(pl.multiple_of(g * GROUP, GROUP), GROUP)
        k = kbuf[at].reshape(GROUP * CACHE, HD)
        v = vbuf[at].reshape(GROUP * CACHE, HD)
        length = jnp.zeros((1, GROUP * CACHE), jnp.int32)
        for s in range(GROUP):
            length = jnp.where(col_row // CACHE == s, lens[g * GROUP + s], length)
        live = same & (col_row % CACHE < length)
        for t in range(STEPS):
            q = block_queries(g, t)
            scores = lax.dot_general(q, k, NT, preferred_element_type=jnp.float32) * scale
            scores = jnp.where(live, scores, NEG)
            top = jnp.max(scores, axis=1, keepdims=True)
            w = jnp.exp(scores - top)
            total = jnp.sum(w, axis=1, keepdims=True)
            mixed = jnp.dot(w.astype(jnp.bfloat16), v, preferred_element_type=jnp.float32)
            to = pl.ds(t * QPK * GROUP, QPK * GROUP)
            acc[g, to] = mixed
            top_ref[g, to] = jnp.broadcast_to(top, (QPK * GROUP, HD))
            sum_ref[g, to] = jnp.broadcast_to(total, (QPK * GROUP, HD))
        return 0

    for copy in p0:
        copy.wait_recv()
    owner_here = owner[core]
    owner_chip, owner_core = owner_here // 2, owner_here % 2
    for b in range(LANES):
        if b < LANES - 1:
            own = down[mine, b * 128 : (b + 1) * 128]
        else:
            own = up[mine, :]
        kept = jnp.where(owner_core == core, own, other[:, b * 128 : (b + 1) * 128])
        half[b * 4 : b * 4 + 4] = kept.reshape(4, 16, 128)

    def piece_to(k):
        return remote(half.at[k], bins.at[chip], p1_send.at[k], p1_recv.at[chip], k * 2 + core, tp)

    def piece_from(k):
        return remote(half.at[0], bins.at[k], p1_send.at[0], p1_recv.at[k], k * 2 + core, tp)

    def send_piece(d, _):
        k = lax.rem(chip + d, CHIPS)

        @pl.when(k < PIECES)
        def _():
            piece_to(k).start()

        return 0

    lax.fori_loop(1, CHIPS, send_piece, 0)

    loads[2].wait()
    loads[3].wait()
    lax.fori_loop(0, 1, cached, 0)

    def spread_to(k):
        return remote(full.at[core, chip], full.at[core, chip], p2_send.at[k], p2_recv.at[chip], k * 2 + core, tp)

    @pl.when(chip < PIECES)
    def _():
        bins[chip] = half[chip]

        def wait_piece(d, _):
            piece_from(lax.rem(chip + d, CHIPS)).wait_recv()
            return 0

        lax.fori_loop(1, CHIPS, wait_piece, 0)
        full[core, chip] = bins[owner_chip]

        def send_out(d, _):
            spread_to(lax.rem(chip + d, CHIPS)).start()
            return 0

        lax.fori_loop(1, CHIPS, send_out, 0)

    lax.fori_loop(1, 2, cached, 0)
    spread(0)
    spread(1)

    def wait_out(d, _):
        k = lax.rem(chip + d, CHIPS)

        @pl.when(k < PIECES)
        def _():
            remote(half.at[0], full.at[core, k], p2_send.at[0], p2_recv.at[k], k * 2 + core, tp).wait_recv()

        return 0

    lax.fori_loop(1, CHIPS, wait_out, 0)

    p3 = remote(full.at[core], full.at[core], p3_send, p3_recv, twin, tp)
    p3.start()

    spread_again(0)
    lax.fori_loop(2, 3, cached, 0)
    spread(2)
    spread_again(1)
    lax.fori_loop(3, 4, cached, 0)
    loads[0].wait()
    loads[1].wait()

    projected = None
    for c in range(NC):
        if c + 3 < NC:
            spread(c + 3)
        if c + 2 < NC:
            spread_again(c + 2)
        complete(c)
        part = jnp.dot(
            gathered[c].reshape(TP * TOK, CHUNK), weights[c * CHUNK : (c + 1) * CHUNK],
            preferred_element_type=jnp.float32,
        )
        projected = part if projected is None else projected + part

    remote(full.at[1 - core], full.at[1 - core], p3_send, p3_recv, twin, tp).wait_recv()
    down_now = jnp.concatenate(
        [full[:, b * 4 : b * 4 + 4].reshape(2 * R, 128) for b in range(LANES - 1)], axis=1
    )
    up_now = full[:, 4 * LANES - 4 : 4 * LANES].reshape(2 * R, HD)
    low_part[...] = lax.dot_general(
        gathered[tp].reshape(TP * TOK, CHUNK), down_now, NT, preferred_element_type=jnp.float32
    ).reshape(TP, TOK, 2 * R)

    def low_to(d):
        q = lax.rem(tp + d, TP)
        return remote(low_part.at[q], low_bins.at[tp], l_send.at[q], l_recv.at[tp], roll, q)

    def low_from(d):
        q = lax.rem(tp + d, TP)
        return remote(low_part.at[q], low_bins.at[q], l_send.at[q], l_recv.at[q], roll, q)

    def all_to(d):
        q = lax.rem(tp + d, TP)
        return remote(low_all.at[tp], low_all.at[tp], g_send.at[q], g_recv.at[tp], roll, q)

    def all_from(d):
        q = lax.rem(tp + d, TP)
        return remote(low_all.at[q], low_all.at[q], g_send.at[q], g_recv.at[q], roll, q)

    for d in range(1, TP):
        low_to(d).start()
    low_bins[tp] = low_part[tp]
    for d in range(1, TP):
        low_from(d).wait_recv()
    low_all[tp] = jnp.sum(low_bins[...], axis=0)
    for d in range(1, TP):
        all_to(d).start()
    for d in range(1, TP):
        all_from(d).wait_recv()

    low = low_all[...].reshape(TP * TOK, 2 * R)
    low_high = low.astype(jnp.bfloat16)
    low_rest = (low - low_high.astype(jnp.float32)).astype(jnp.bfloat16)
    zero = jnp.zeros((R, HD), jnp.bfloat16)
    up_both = jnp.concatenate(
        [jnp.concatenate([up_now[:R], zero], axis=0), jnp.concatenate([zero, up_now[R:]], axis=0)], axis=1
    )
    projected = projected + (
        jnp.dot(low_high, up_both, preferred_element_type=jnp.float32)
        + jnp.dot(low_rest, up_both, preferred_element_type=jnp.float32)
    )
    fresh = projected.astype(jnp.bfloat16)

    span = GROUP * STEPS
    row2 = lax.broadcasted_iota(jnp.int32, (ROWS, span), 0)
    col2 = lax.broadcasted_iota(jnp.int32, (ROWS, span), 1)
    sample2 = col2 // TOK * (GROUP // 2) + col2 % (GROUP // 2)
    step2 = col2 % TOK // (GROUP // 2)
    live2 = (row2 % GROUP == sample2) & (step2 <= row2 // (QPK * GROUP))
    for g in range(GROUPS):
        q = jnp.concatenate([block_queries(g, t) for t in range(STEPS)], axis=0)
        k = fresh[g * span : (g + 1) * span, :HD]
        v = fresh[g * span : (g + 1) * span, HD:]
        scores = lax.dot_general(q, k, NT, preferred_element_type=jnp.float32) * scale
        scores = jnp.where(live2, scores, NEG)
        old_top = top_ref[g]
        top = jnp.maximum(old_top, jnp.max(scores, axis=1, keepdims=True))
        w = jnp.exp(scores - top[:, :span])
        fade = jnp.exp(old_top - top)
        total = sum_ref[g] * fade + jnp.sum(w, axis=1, keepdims=True)
        mixed = acc[g] * fade + jnp.dot(w.astype(jnp.bfloat16), v, preferred_element_type=jnp.float32)
        done = (mixed / total).astype(jnp.bfloat16)
        for t in range(STEPS):
            for j in range(QPK):
                at = (t * QPK + j) * GROUP
                out[t, g * GROUP : (g + 1) * GROUP, j * HD : (j + 1) * HD] = done[at : at + GROUP]

    for copy in p0:
        copy.wait_send()
    p3.wait_send()
    for copy in sends:
        copy.wait_send()
    for d in range(1, TP):
        low_to(d).wait_send()
        all_to(d).wait_send()

    def sent_piece(d, _):
        k = lax.rem(chip + d, CHIPS)

        @pl.when(k < PIECES)
        def _():
            piece_to(k).wait_send()

        return 0

    lax.fori_loop(1, CHIPS, sent_piece, 0)

    @pl.when(chip < PIECES)
    def _():
        def sent_out(d, _):
            spread_to(lax.rem(chip + d, CHIPS)).wait_send()
            return 0

        lax.fori_loop(1, CHIPS, sent_out, 0)


def local(hidden, queries, key_cache, value_cache, cache_len, base_key, base_value, factor_a, factor_b, owner):
    down = jnp.swapaxes(factor_a[0], 1, 2).reshape(2 * R, CHUNK)
    up = factor_b[0].reshape(2 * R, HD)
    vmem = pl.BlockSpec(memory_space=pltpu.VMEM)
    smem = pl.BlockSpec(memory_space=pltpu.SMEM)
    hbm = pl.BlockSpec(memory_space=pl.ANY)
    dma = pltpu.SemaphoreType.DMA
    return pl.pallas_call(
        kernel,
        out_shape=jax.ShapeDtypeStruct((STEPS, SAMP, QPK * HD), jnp.bfloat16),
        in_specs=[smem, smem, hbm, vmem, hbm, hbm, hbm, hbm, vmem, vmem],
        out_specs=vmem,
        scratch_shapes=[
            pltpu.VMEM((NC, TP, TOK, CHUNK), jnp.bfloat16),
            pltpu.VMEM((D, 2 * HD), jnp.bfloat16),
            pltpu.VMEM((SAMP, CACHE, HD), jnp.bfloat16),
            pltpu.VMEM((SAMP, CACHE, HD), jnp.bfloat16),
            pltpu.VMEM((PIECES, 16, 128), jnp.bfloat16),
            pltpu.VMEM((R, CHUNK + HD), jnp.bfloat16),
            pltpu.VMEM((CHIPS, 16, 128), jnp.bfloat16),
            pltpu.VMEM((2, PIECES, 16, 128), jnp.bfloat16),
            pltpu.VMEM((GROUPS, ROWS, HD), jnp.float32),
            pltpu.VMEM((GROUPS, ROWS, HD), jnp.float32),
            pltpu.VMEM((GROUPS, ROWS, HD), jnp.float32),
            pltpu.VMEM((TP, TOK, 2 * R), jnp.float32),
            pltpu.VMEM((TP, TOK, 2 * R), jnp.float32),
            pltpu.VMEM((TP, TOK, 2 * R), jnp.float32),
            dma((4 + NC,)),
            dma((2,)), dma((2,)),
            dma((PIECES,)), dma((CHIPS,)),
            dma((CHIPS,)), dma((PIECES,)),
            dma, dma,
            dma((NC, 9)), dma((NC, 9)),
            dma((TP,)), dma((TP,)), dma((TP,)), dma((TP,)),
        ],
        compiler_params=pltpu.CompilerParams(
            collective_id=0, has_side_effects=True, vmem_limit_bytes=48 * 1024 * 1024
        ),
    )(
        owner, cache_len, hidden.reshape(STEPS * SAMP // TP, D), queries, key_cache, value_cache,
        base_key, base_value, down, up,
    )


def solution(mesh):
    placed = (
        P(None, ("roll", "tp"), None),
        P(None, "roll", "tp"),
        P("roll", None, "tp"),
        P("roll", None, "tp"),
        P("roll"),
        P(None, "tp"),
        P(None, "tp"),
        P("roll", None, "tp", None),
        P("roll", None, None, "tp"),
        P(),
    )
    return jax.shard_map(
        local, mesh=mesh, in_specs=placed, out_specs=P(None, "roll", "tp"), check_vma=False
    )
```

time: 611 us -> 83.3 us (0.14)
  the two profiles are of different devices: /device:TPU:1 before, /device:TPU:64 now
where the time goes in v1:
time: 83.3 us; the launch traced here: 82.8 us
  Pallas kernels  72.5 us (87%)
  local copies, waits for them, and re-layouts  10.3 us (12%)
    pallas_call x1, Pallas kernels, local(): pl.pallas_call(kernel, out_shape=jax.ShapeDtypeStruct((STEPS, SAMP, QPK *...  72.5 us
    unnamed x21, local copies, waits for them, and re-layouts  10.3 us

profile of v1, /device:TPU:64, one launch (start us, length us, event | category | flops | bytes accessed | tf_op | source)
XLA Modules:
  0.0 82.8 jit_solution(16981400483970128274)
XLA Ops:
  0.0 0.0 copy-start
  0.0 1.3 %copy-done = bf16[5120,128]{1,0:T(8,128)(2,1)S(1)} copy-done((bf16[5120,128]{1,0:T(8,128)(2,1)S(1)}, bf16[5120,128]{1,0:T(8,128)(2,1)}, u32[]{:S(2)}) %copy-start) | copy-done | bytes 1310744
  1.3 0.0 copy-start.1
  1.3 1.3 %copy-done.1 = bf16[5120,128]{1,0:T(8,128)(2,1)S(1)} copy-done((bf16[5120,128]{1,0:T(8,128)(2,1)S(1)}, bf16[5120,128]{1,0:T(8,128)(2,1)}, u32[]{:S(2)}) %copy-start.1) | copy-done | bytes 1310744
  2.6 0.0 copy-start.2
  2.6 1.0 %copy-done.2 = bf16[64,32,128]{2,1,0:T(8,128)(2,1)S(1)} copy-done((bf16[64,32,128]{2,1,0:T(8,128)(2,1)S(1)}, bf16[64,32,128]{2,1,0:T(8,128)(2,1)}, u32[]{:S(2)}) %copy-start.2) | copy-done | bytes 524312
  3.7 0.0 copy-start.3
  3.7 1.0 %copy-done.3 = bf16[64,32,128]{2,1,0:T(8,128)(2,1)S(1)} copy-done((bf16[64,32,128]{2,1,0:T(8,128)(2,1)S(1)}, bf16[64,32,128]{2,1,0:T(8,128)(2,1)}, u32[]{:S(2)}) %copy-start.3) | copy-done | bytes 524312
  4.7 0.0 copy-start.4
  4.7 1.0 %copy-done.4 = bf16[4,8,5120]{2,1,0:T(8,128)(2,1)S(1)} copy-done((bf16[4,8,5120]{2,1,0:T(8,128)(2,1)S(1)}, bf16[4,8,5120]{2,1,0:T(8,128)(2,1)}, u32[]{:S(2)}) %copy-start.4) | copy-done | bytes 327704
  5.7 0.0 copy-start.5
  5.7 0.9 %copy-done.5 = bf16[4,64,512]{2,1,0:T(8,128)(2,1)S(1)} copy-done((bf16[4,64,512]{2,1,0:T(8,128)(2,1)S(1)}, bf16[4,64,512]{2,1,0:T(8,128)(2,1)}, u32[]{:S(2)}) %copy-start.5) | copy-done | bytes 262168
  6.6 0.0 copy-start.6
  6.6 0.9 %copy-done.6 = bf16[1,2,640,64]{2,3,1,0:T(8,128)(2,1)S(1)} copy-done((bf16[1,2,640,64]{2,3,1,0:T(8,128)(2,1)S(1)}, bf16[1,2,640,64]{2,3,1,0:T(8,128)(2,1)}, u32[]{:S(2)}) %copy-start.6) | copy-done | bytes 163864
  7.6 0.0 copy-start.7
  7.6 0.8 copy-done.7
  8.3 0.0 copy-start.8
  8.3 0.7 copy-done.8
  9.0 0.0 copy-start.9
  9.0 0.7 copy-done.9
  9.6 72.5 %shard_map.100 = bf16[4,64,512]{2,1,0:T(8,128)(2,1)S(1)} custom-call(s32[2]{0:T(128)S(1)} %copy-done.8, s32[64]{0:T(128)S(1)} %copy-done.9, bf16[32,5120]{1,0:T(8,128)(2,1)S(1)} %bitcast.7, bf16[4,64,512]{2,1,0:T(8,128)(2,1)S(1)} %copy-done.5, bf16[64,32,128]{2,1,0:T(8,128)(2,1)S(1)} %copy-done.2, bf16[64,32,128]{2,1,0:T(8,128)(2,1)S(1)} %copy-done.3, ...), custom_call_target="tpu_custom_call" | custom-call | tf_op jit(solution)/shard_map/pallas_call | solution.py:372
  82.1 0.7 copy.12
Async XLA Ops:
  0.0 1.3 %copy-start = (bf16[5120,128]{1,0:T(8,128)(2,1)S(1)}, bf16[5120,128]{1,0:T(8,128)(2,1)}, u32[]{:S(2)}) copy-start(bf16[5120,128]{1,0:T(8,128)(2,1)} %base_key.1) | copy-start | bytes 3932164
  1.3 1.3 %copy-start.1 = (bf16[5120,128]{1,0:T(8,128)(2,1)S(1)}, bf16[5120,128]{1,0:T(8,128)(2,1)}, u32[]{:S(2)}) copy-start(bf16[5120,128]{1,0:T(8,128)(2,1)} %base_value.1) | copy-start | bytes 3932164
  2.6 1.0 %copy-start.2 = (bf16[64,32,128]{2,1,0:T(8,128)(2,1)S(1)}, bf16[64,32,128]{2,1,0:T(8,128)(2,1)}, u32[]{:S(2)}) copy-start(bf16[64,32,128]{2,1,0:T(8,128)(2,1)} %keys.1) | copy-start | bytes 1572868
  3.7 1.0 %copy-start.3 = (bf16[64,32,128]{2,1,0:T(8,128)(2,1)S(1)}, bf16[64,32,128]{2,1,0:T(8,128)(2,1)}, u32[]{:S(2)}) copy-start(bf16[64,32,128]{2,1,0:T(8,128)(2,1)} %values.1) | copy-start | bytes 1572868
  4.7 1.0 %copy-start.4 = (bf16[4,8,5120]{2,1,0:T(8,128)(2,1)S(1)}, bf16[4,8,5120]{2,1,0:T(8,128)(2,1)}, u32[]{:S(2)}) copy-start(bf16[4,8,5120]{2,1,0:T(8,128)(2,1)} %param.10) | copy-start | bytes 983044
  5.7 0.9 %copy-start.5 = (bf16[4,64,512]{2,1,0:T(8,128)(2,1)S(1)}, bf16[4,64,512]{2,1,0:T(8,128)(2,1)}, u32[]{:S(2)}) copy-start(bf16[4,64,512]{2,1,0:T(8,128)(2,1)} %queries.1) | copy-start | bytes 786436
  6.6 0.9 %copy-start.6 = (bf16[1,2,640,64]{2,3,1,0:T(8,128)(2,1)S(1)}, bf16[1,2,640,64]{2,3,1,0:T(8,128)(2,1)}, u32[]{:S(2)}) copy-start(bf16[1,2,640,64]{2,3,1,0:T(8,128)(2,1)} %param.17) | copy-start | bytes 491524
  7.6 0.8 copy-start.7
  8.3 0.7 copy-start.8
  9.0 0.7 copy-start.9

commit v2 on v1

v2 whole, which is shorter than its diff:
```python
import math

import jax
import jax.numpy as jnp
from jax import lax
from jax.experimental import pallas as pl
from jax.experimental.pallas import tpu as pltpu
from jax.sharding import PartitionSpec as P

D = 5120
HD = 128
QPK = 4
R = 64
STEPS = 4
SAMP = 64
CACHE = 32
TP = 8
ROWS_TP = D // TP
RANK = 2 * R // TP
NC = 4
CHUNK = D // NC
TOK = STEPS * SAMP // TP
CHIPS = 32
REDUCERS = 8
GROUP = 16
GROUPS = SAMP // GROUP
ROWS = STEPS * QPK * GROUP
NEG = -1e30
MESH = pl.DeviceIdType.MESH
NT = (((1,), (1,)), ((), ()))
TN = (((0,), (0,)), ((), ()))


def kernel(
    owner_hbm, lens_hbm, hidden, queries_hbm, keys, values, base_key, base_value, down_hbm, up_hbm, out,
    owner, lens, queries, down, up,
    gathered, weights, kbuf, vbuf, down_other, up_other, down_half, up_half, down_bins, up_bins, down_now, up_now,
    acc, top_ref, sum_ref, low_all,
    load_sem, p0_send, p0_recv, p1_send, p1_recv, p2_send, p2_recv, p3_send, p3_recv,
    h_send, h_recv, g_send, g_recv, go_sem,
):
    roll, tp = lax.axis_index("roll"), lax.axis_index("tp")
    y_hi, z, core = roll // 16, roll // 2 % 8, roll % 2
    chip = (z // 4) * 16 + y_hi * 4 + z % 4
    x, y = tp // 2, tp % 2
    pos = lambda px, py: lax.rem(px + 8, 4) * 2 + py
    def roll_of(k, c):
        return (k // 4 % 4) * 16 + ((k // 16) * 4 + k % 4) * 2 + c

    right, left, across = pos(x + 1, y), pos(x - 1, y), pos(x, 1 - y)
    twin = roll + 1 - 2 * core
    down_core = tp // 4
    has_down = core == down_core
    reduces = chip < REDUCERS
    late = chip >= CHIPS // 2
    partner = roll_of(lax.rem(chip + CHIPS // 2, CHIPS), core)
    picked = lax.rem(chip + TP - tp, TP)

    def remote(src, dst, send, recv, to_roll, to_tp):
        return pltpu.make_async_remote_copy(
            src_ref=src, dst_ref=dst, send_sem=send, recv_sem=recv,
            device_id=(to_roll, to_tp), device_id_type=MESH,
        )

    loads = [
        pltpu.make_async_copy(src, dst, load_sem.at[k])
        for k, (src, dst) in enumerate(
            [
                (down_hbm, down), (up_hbm, up), (owner_hbm, owner), (lens_hbm, lens), (queries_hbm, queries),
                (keys, kbuf), (values, vbuf),
                (base_key, weights.at[:, pl.ds(0, HD)]), (base_value, weights.at[:, pl.ds(HD, HD)]),
            ]
            + [(hidden.at[:, pl.ds(c * CHUNK, CHUNK)], gathered.at[c, tp]) for c in range(NC)]
        )
    ]
    for copy in loads:
        copy.start()

    barrier = pltpu.get_barrier_semaphore()

    def greet(to_roll, to_tp):
        pl.semaphore_signal(barrier, inc=1, device_id=(to_roll, to_tp), device_id_type=MESH)

    greet(twin, tp)

    def greet_tp(d, _):
        greet(roll, lax.rem(tp + d, TP))
        return 0

    lax.fori_loop(1, TP, greet_tp, 0)

    @pl.when(reduces)
    def _():
        def greet_sender(k, _):
            greet(roll_of(k, jnp.where(has_down, core, chip // 4)), jnp.where(has_down, picked, tp))
            return 0

        lax.fori_loop(CHIPS // 2, CHIPS, greet_sender, 0)

    @pl.when(jnp.logical_not(late))
    def _():
        greet(partner, tp)

    pl.semaphore_wait(barrier, jnp.where(late, TP + TP + 1, TP))

    @pl.when(late)
    def _():
        pl.semaphore_signal(go_sem, inc=1, device_id=(partner, tp), device_id_type=MESH)

    own_down = has_down & reduces & (picked == tp)
    own_up = (core != down_core) & reduces & (chip // 4 == core)
    mine = pl.ds(pl.multiple_of(core * R, R), R)
    theirs = pl.ds(pl.multiple_of((1 - core) * R, R), R)
    p0 = [
        remote(down_hbm.at[theirs], down_other, p0_send.at[0], p0_recv.at[0], twin, tp),
        remote(up_hbm.at[theirs], up_other, p0_send.at[1], p0_recv.at[1], twin, tp),
    ]
    for copy in p0:
        copy.start()
    for copy in loads[:3]:
        copy.wait()
    owner_core = owner[core] % 2
    for copy in p0:
        copy.wait_recv()
    down_half[...] = jnp.where(owner_core == core, down[mine, :], down_other[...]).reshape(4, RANK, ROWS_TP)
    up_half[...] = jnp.where(owner_core == core, up[mine, :], up_other[...]).reshape(4, RANK, HD)

    def down_to(a):
        return remote(
            down_half.at[a], down_bins.at[chip], p1_send.at[a], p1_recv.at[chip],
            roll_of(lax.rem(tp + 4 * core + a, TP), core), 4 * core + a,
        )

    def up_to(a):
        return remote(
            up_half.at[a], up_bins.at[chip], p1_send.at[4 + a], p1_recv.at[chip], roll_of(4 * core + a, 1 - down_core), tp
        )

    def is_own_down(a):
        return own_down & (4 * core + a == tp)

    def is_own_up(a):
        return own_up & (4 * core + a == chip)

    def send_pieces():
        for a in range(4):
            @pl.when(jnp.logical_not(is_own_down(a)))
            def _():
                down_to(a).start()

            @pl.when(jnp.logical_not(is_own_up(a)))
            def _():
                up_to(a).start()

            @pl.when(is_own_down(a))
            def _():
                down_bins[chip] = down_half[a]

            @pl.when(is_own_up(a))
            def _():
                up_bins[chip] = up_half[a]

    def hop(c, kind, block, to, src=None, rows=None):
        dst = gathered.at[c, block]
        if rows is not None:
            dst = dst.at[rows]
        return remote(dst if src is None else src, dst, h_send.at[c, kind], h_recv.at[c, kind], roll, to)

    sends = []

    def start(copy):
        copy.start()
        sends.append(copy)

    def landed(c, kind, block, rows=None):
        hop(c, kind, block, across, rows=rows).wait_recv()

    top_rows, low_rows = pl.ds(0, TOK // 2), pl.ds(TOK // 2, TOK // 2)
    far, far_across = pos(x + 2, y), pos(x + 2, 1 - y)
    left_across, right_across = pos(x - 1, 1 - y), pos(x + 1, 1 - y)
    along_y = (0, 1)
    along_x = (2, 3)

    def pass_on(c):
        landed(c, 1, left)
        start(hop(c, 5, left, right, rows=top_rows))
        if c in along_x:
            start(hop(c, 3, left, across))
        landed(c, 2, right)
        start(hop(c, 6, right, left, rows=low_rows))
        if c in along_x:
            start(hop(c, 4, right, across))

    def spread(c):
        landed(c, 0, across)
        start(hop(c, 3, across, right))
        start(hop(c, 4, across, left))
        pass_on(c)

    def spread_again(c):
        landed(c, 3, left_across)
        start(hop(c, 7, left_across, right, rows=top_rows))
        landed(c, 4, right_across)
        start(hop(c, 8, right_across, left, rows=low_rows))

    def far_across_y(c):
        landed(c, 5, far, top_rows)
        landed(c, 6, far, low_rows)
        start(hop(c, 7, far, across))

    scale = 1.0 / math.sqrt(HD)
    row = lax.broadcasted_iota(jnp.int32, (QPK * GROUP, GROUP * CACHE), 0)
    col = lax.broadcasted_iota(jnp.int32, (QPK * GROUP, GROUP * CACHE), 1)
    same = (row % GROUP) == (col // CACHE)
    col_row = lax.broadcasted_iota(jnp.int32, (1, GROUP * CACHE), 1)

    def block_queries(g, t):
        at = pl.ds(pl.multiple_of(g * GROUP, GROUP), GROUP)
        return jnp.concatenate([queries[t, at, j * HD : (j + 1) * HD] for j in range(QPK)], axis=0)

    def cached(g, _):
        at = pl.ds(pl.multiple_of(g * GROUP, GROUP), GROUP)
        k = kbuf[at].reshape(GROUP * CACHE, HD)
        v = vbuf[at].reshape(GROUP * CACHE, HD)
        length = jnp.zeros((1, GROUP * CACHE), jnp.int32)
        for s in range(GROUP):
            length = jnp.where(col_row // CACHE == s, lens[g * GROUP + s], length)
        live = same & (col_row % CACHE < length)
        for t in range(STEPS):
            q = block_queries(g, t)
            scores = lax.dot_general(q, k, NT, preferred_element_type=jnp.float32) * scale
            scores = jnp.where(live, scores, NEG)
            top = jnp.max(scores, axis=1, keepdims=True)
            w = jnp.exp(scores - top)
            total = jnp.sum(w, axis=1, keepdims=True)
            mixed = jnp.dot(w.astype(jnp.bfloat16), v, preferred_element_type=jnp.float32)
            to = pl.ds(t * QPK * GROUP, QPK * GROUP)
            acc[g, to] = mixed
            top_ref[g, to] = jnp.broadcast_to(top, (QPK * GROUP, HD))
            sum_ref[g, to] = jnp.broadcast_to(total, (QPK * GROUP, HD))
        return 0

    @pl.when(late)
    def _():
        send_pieces()

    for copy in loads[3:7]:
        copy.wait()
    lax.fori_loop(0, jnp.where(late, GROUPS, 0), cached, 0)
    for c in along_x + along_y:
        own = hidden.at[:, pl.ds(c * CHUNK, CHUNK)]
        start(hop(c, 0, tp, across, own))
        start(hop(c, 1, tp, right, own))
        start(hop(c, 2, tp, left, own))

    lax.fori_loop(jnp.where(late, GROUPS, 0), GROUPS, cached, 0)
    for c in along_x:
        pass_on(c)
    for c in along_y:
        spread(c)

    @pl.when(jnp.logical_not(late))
    def _():
        pl.semaphore_wait(go_sem, 1)
        send_pieces()

    for c in along_x:
        far_across_y(c)
    for c in along_y:
        spread_again(c)

    for copy in loads[7:]:
        copy.wait()
    projected = None
    for c in along_y + along_x:
        if c in along_y:
            landed(c, 5, far, top_rows)
            landed(c, 6, far, low_rows)
            landed(c, 7, far_across, top_rows)
            landed(c, 8, far_across, low_rows)
        else:
            landed(c, 0, across)
            landed(c, 3, left_across)
            landed(c, 4, right_across)
            landed(c, 7, far_across)
        part = jnp.dot(
            gathered[c].reshape(TP * TOK, CHUNK), weights[c * CHUNK : (c + 1) * CHUNK],
            preferred_element_type=jnp.float32,
        )
        projected = part if projected is None else projected + part

    def down_out(k):
        return remote(down_now.at[picked], down_now.at[picked], p2_send.at[k], p2_recv.at[picked], roll_of(k, core), tp)

    def up_out(k):
        return remote(up_now.at[chip], up_now.at[chip], p2_send.at[k], p2_recv.at[chip], roll_of(k, core), tp)

    @pl.when(reduces & has_down)
    def _():
        def wait_piece(k, _):
            @pl.when((k != chip) | (tp != picked))
            def _():
                remote(down_half.at[0], down_bins.at[k], p1_send.at[0], p1_recv.at[k], twin, tp).wait_recv()

            return 0

        lax.fori_loop(0, CHIPS, wait_piece, 0)
        source = owner[core] // 2
        down_now[picked] = down_bins[(source % 8) // 4 * 16 + source // 8 * 4 + source % 4]

        def send_out(k, _):
            @pl.when(k != chip)
            def _():
                down_out(k).start()

            return 0

        lax.fori_loop(0, CHIPS, send_out, 0)

    @pl.when(reduces & (core != down_core))
    def _():
        def wait_piece(k, _):
            @pl.when((k != chip) | (chip // 4 != core))
            def _():
                remote(up_half.at[0], up_bins.at[k], p1_send.at[4], p1_recv.at[k], twin, tp).wait_recv()

            return 0

        lax.fori_loop(0, CHIPS, wait_piece, 0)
        source = owner[chip // 4] // 2
        up_now[chip] = up_bins[(source % 8) // 4 * 16 + source // 8 * 4 + source % 4]

        def send_out(k, _):
            @pl.when(k != chip)
            def _():
                up_out(k).start()

            return 0

        lax.fori_loop(0, CHIPS, send_out, 0)

    p3_down = remote(down_now, down_now, p3_send, p3_recv, twin, tp)
    p3_up = remote(up_now, up_now, p3_send, p3_recv, twin, tp)

    @pl.when(has_down)
    def _():
        for k in range(REDUCERS):
            @pl.when((k != picked) | (chip >= REDUCERS))
            def _():
                remote(down_half.at[0], down_now.at[k], p1_send.at[0], p2_recv.at[k], twin, tp).wait_recv()
        p3_down.start()
        p3_up.wait_recv()

    @pl.when(core != down_core)
    def _():
        for k in range(REDUCERS):
            @pl.when(k != chip)
            def _():
                remote(up_half.at[0], up_now.at[k], p1_send.at[4], p2_recv.at[k], twin, tp).wait_recv()
        p3_up.start()
        p3_down.wait_recv()

    low = None
    for c in range(NC):
        rows = jnp.concatenate(
            [down_now[k] for k in range(c * CHUNK // ROWS_TP, (c + 1) * CHUNK // ROWS_TP)], axis=1
        )
        part = lax.dot_general(
            rows, gathered[c].reshape(TP * TOK, CHUNK), NT, preferred_element_type=jnp.float32
        )
        low = part if low is None else low + part
    low_all[tp] = low.astype(jnp.bfloat16)

    def all_to(d):
        q = lax.rem(tp + d, TP)
        return remote(low_all.at[tp], low_all.at[tp], g_send.at[q], g_recv.at[tp], roll, q)

    def all_from(d):
        q = lax.rem(tp + d, TP)
        return remote(low_all.at[q], low_all.at[q], g_send.at[q], g_recv.at[q], roll, q)

    for d in range(1, TP):
        all_to(d).start()
    zero = jnp.zeros((R, HD), jnp.bfloat16)
    up_rows = up_now[...].reshape(2 * R, HD)
    up_both = jnp.concatenate(
        [jnp.concatenate([up_rows[:R], zero], axis=0), jnp.concatenate([zero, up_rows[R:]], axis=0)], axis=1
    )
    for d in range(1, TP):
        all_from(d).wait_recv()
    projected = projected + lax.dot_general(
        low_all[...].reshape(2 * R, TP * TOK), up_both, TN, preferred_element_type=jnp.float32
    )
    fresh = projected.astype(jnp.bfloat16)

    span = GROUP * STEPS
    row2 = lax.broadcasted_iota(jnp.int32, (ROWS, span), 0)
    col2 = lax.broadcasted_iota(jnp.int32, (ROWS, span), 1)
    sample2 = col2 // TOK * (GROUP // 2) + col2 % (GROUP // 2)
    step2 = col2 % TOK // (GROUP // 2)
    live2 = (row2 % GROUP == sample2) & (step2 <= row2 // (QPK * GROUP))
    for g in range(GROUPS):
        q = jnp.concatenate([block_queries(g, t) for t in range(STEPS)], axis=0)
        k = fresh[g * span : (g + 1) * span, :HD]
        v = fresh[g * span : (g + 1) * span, HD:]
        scores = lax.dot_general(q, k, NT, preferred_element_type=jnp.float32) * scale
        scores = jnp.where(live2, scores, NEG)
        old_top = top_ref[g]
        top = jnp.maximum(old_top, jnp.max(scores, axis=1, keepdims=True))
        w = jnp.exp(scores - top[:, :span])
        fade = jnp.exp(old_top - top)
        total = sum_ref[g] * fade + jnp.sum(w, axis=1, keepdims=True)
        mixed = acc[g] * fade + jnp.dot(w.astype(jnp.bfloat16), v, preferred_element_type=jnp.float32)
        done = (mixed / total).astype(jnp.bfloat16)
        for t in range(STEPS):
            for j in range(QPK):
                at = (t * QPK + j) * GROUP
                out[t, g * GROUP : (g + 1) * GROUP, j * HD : (j + 1) * HD] = done[at : at + GROUP]

    for copy in p0 + sends:
        copy.wait_send()
    for d in range(1, TP):
        all_to(d).wait_send()
    for a in range(4):
        @pl.when(jnp.logical_not(is_own_down(a)))
        def _():
            down_to(a).wait_send()

        @pl.when(jnp.logical_not(is_own_up(a)))
        def _():
            up_to(a).wait_send()

    @pl.when(has_down)
    def _():
        p3_down.wait_send()

    @pl.when(core != down_core)
    def _():
        p3_up.wait_send()

    @pl.when(reduces & has_down)
    def _():
        def sent_out(d, _):
            down_out(lax.rem(chip + d, CHIPS)).wait_send()
            return 0

        lax.fori_loop(1, CHIPS, sent_out, 0)

    @pl.when(reduces & (core != down_core))
    def _():
        def sent_out(d, _):
            up_out(lax.rem(chip + d, CHIPS)).wait_send()
            return 0

        lax.fori_loop(1, CHIPS, sent_out, 0)


def local(hidden, queries, key_cache, value_cache, cache_len, base_key, base_value, factor_a, factor_b, owner):
    down = jnp.swapaxes(factor_a[0], 1, 2).reshape(2 * R, ROWS_TP)
    up = factor_b[0].reshape(2 * R, HD)
    hbm = pl.BlockSpec(memory_space=pltpu.HBM)
    dma = pltpu.SemaphoreType.DMA
    vmem, bf16, f32 = pltpu.VMEM, jnp.bfloat16, jnp.float32
    return pl.pallas_call(
        kernel,
        out_shape=jax.ShapeDtypeStruct((STEPS, SAMP, QPK * HD), jnp.bfloat16),
        in_specs=[hbm] * 10,
        out_specs=pl.BlockSpec(memory_space=pltpu.VMEM),
        scratch_shapes=[
            pltpu.SMEM((2,), jnp.int32),
            pltpu.SMEM((SAMP,), jnp.int32),
            vmem((STEPS, SAMP, QPK * HD), bf16),
            vmem((2 * R, ROWS_TP), bf16),
            vmem((2 * R, HD), bf16),
            vmem((NC, TP, TOK, CHUNK), bf16),
            vmem((D, 2 * HD), bf16),
            vmem((SAMP, CACHE, HD), bf16),
            vmem((SAMP, CACHE, HD), bf16),
            vmem((R, ROWS_TP), bf16),
            vmem((R, HD), bf16),
            vmem((4, RANK, ROWS_TP), bf16),
            vmem((4, RANK, HD), bf16),
            vmem((CHIPS, RANK, ROWS_TP), bf16),
            vmem((CHIPS, RANK, HD), bf16),
            vmem((REDUCERS, RANK, ROWS_TP), bf16),
            vmem((REDUCERS, RANK, HD), bf16),
            vmem((GROUPS, ROWS, HD), f32),
            vmem((GROUPS, ROWS, HD), f32),
            vmem((GROUPS, ROWS, HD), f32),
            vmem((TP, RANK, TP * TOK), bf16),
            dma((9 + NC,)),
            dma((2,)), dma((2,)),
            dma((8,)), dma((CHIPS,)),
            dma((CHIPS,)), dma((REDUCERS,)),
            dma, dma,
            dma((NC, 9)), dma((NC, 9)),
            dma((TP,)), dma((TP,)),
            pltpu.SemaphoreType.REGULAR,
        ],
        compiler_params=pltpu.CompilerParams(
            collective_id=0, has_side_effects=True, vmem_limit_bytes=63 * 1024 * 1024
        ),
    )(
        owner, cache_len, hidden.reshape(TOK, D), queries, key_cache, value_cache,
        base_key, base_value, down, up,
    )


def solution(mesh):
    placed = (
        P(None, ("roll", "tp"), None),
        P(None, "roll", "tp"),
        P("roll", None, "tp"),
        P("roll", None, "tp"),
        P("roll"),
        P(None, "tp"),
        P(None, "tp"),
        P("roll", None, "tp", None),
        P("roll", None, None, "tp"),
        P(),
    )
    return jax.shard_map(
        local, mesh=mesh, in_specs=placed, out_specs=P(None, "roll", "tp"), check_vma=False
    )
```

time: 83.3 us -> 59.5 us (0.71)
  the two profiles are of different devices: /device:TPU:64 before, /device:TPU:1 now
where the time goes in v2:
time: 59.5 us; the launch traced here: 59.3 us
  Pallas kernels  57.6 us (97%)
  local copies, waits for them, and re-layouts  1.67 us (3%)
    pallas_call x1, Pallas kernels, local(): pl.pallas_call(kernel, out_shape=jax.ShapeDtypeStruct((STEPS, SAMP, QPK *...  57.6 us
    unnamed x1, local copies, waits for them, and re-layouts  1.67 us

profile of v2, /device:TPU:1, one launch (start us, length us, event | category | flops | bytes accessed | tf_op | source)
XLA Modules:
  0.0 59.3 jit_solution(5814670539689542143)
XLA Ops:
  0.0 57.6 %shard_map.100 = bf16[4,64,512]{2,1,0:T(8,128)(2,1)} custom-call(s32[2]{0:T(128)} %owner_hbm.1, s32[64]{0:T(128)} %lens_hbm.1, bf16[32,5120]{1,0:T(8,128)(2,1)} %bitcast.7, bf16[4,64,512]{2,1,0:T(8,128)(2,1)} %queries_hbm.1, bf16[64,32,128]{2,1,0:T(8,128)(2,1)} %keys.1, bf16[64,32,128]{2,1,0:T(8,128)(2,1)} %values.1, bf16[5120,128]{1,0:T(8,128)(2,1)} %base_key.1, ...), custom_call_target="tpu_custom_call" | custom-call | tf_op jit(solution)/shard_map/pallas_call | solution.py:464
  57.6 1.7 %copy.12 = bf16[4,64,512]{2,1,0:T(8,128)(2,1)} copy(bf16[4,64,512]{2,1,0:T(8,128)(2,1)} %shard_map.100) | data formatting | bytes 524288

commit v3 on v2

v3 whole, which is shorter than its diff:
```python
import math

import jax
import jax.numpy as jnp
from jax import lax
from jax.experimental import pallas as pl
from jax.experimental.pallas import tpu as pltpu
from jax.sharding import PartitionSpec as P

D = 5120
HD = 128
QPK = 4
R = 64
STEPS = 4
SAMP = 64
CACHE = 32
TP = 8
ROWS_TP = D // TP
PIECE = 16
WIDTH = ROWS_TP + HD
NC = 4
CHUNK = D // NC
TOK = STEPS * SAMP // TP
ZS = 8
PICKERS = 4
YS = 4
GROUP = 16
GROUPS = SAMP // GROUP
ROWS = STEPS * QPK * GROUP
NEG = -1e30
MESH = pl.DeviceIdType.MESH
NT = (((1,), (1,)), ((), ()))
TN = (((0,), (0,)), ((), ()))


def kernel(
    owner_hbm, lens_hbm, hidden, queries_hbm, keys, values, base_key, base_value, down_hbm, up_hbm, out,
    owner, lens, queries, down, up,
    gathered, weights, kbuf, vbuf, other, half, bins_z, bins_y, now, acc, top_ref, sum_ref, low_all,
    load_sem, p0_send, p0_recv, p1_send, p1_recv, p2_send, p2_recv, p3_send, p3_recv, p4_send, p4_recv,
    h_send, h_recv, g_send, g_recv,
):
    roll, tp = lax.axis_index("roll"), lax.axis_index("tp")
    y_hi, z, core = roll // 16, roll // 2 % 8, roll % 2
    x, y = tp // 2, tp % 2
    pos = lambda px, py: lax.rem(px + 8, 4) * 2 + py
    right, left, across = pos(x + 1, y), pos(x - 1, y), pos(x, 1 - y)
    twin = roll + 1 - 2 * core
    picks = z < PICKERS

    def at_z(to_z):
        return y_hi * 16 + to_z * 2 + core

    def at_y(to_y):
        return to_y * 16 + z * 2 + core

    def remote(src, dst, send, recv, to_roll, to_tp):
        return pltpu.make_async_remote_copy(
            src_ref=src, dst_ref=dst, send_sem=send, recv_sem=recv,
            device_id=(to_roll, to_tp), device_id_type=MESH,
        )

    loads = [
        pltpu.make_async_copy(src, dst, load_sem.at[k])
        for k, (src, dst) in enumerate(
            [
                (down_hbm, down), (up_hbm, up), (owner_hbm, owner), (lens_hbm, lens), (queries_hbm, queries),
                (keys, kbuf), (values, vbuf),
                (base_key, weights.at[:, pl.ds(0, HD)]), (base_value, weights.at[:, pl.ds(HD, HD)]),
            ]
            + [(hidden.at[:, pl.ds(c * CHUNK, CHUNK)], gathered.at[c, tp]) for c in range(NC)]
        )
    ]
    for copy in loads:
        copy.start()

    barrier = pltpu.get_barrier_semaphore()

    def greet(to_roll, to_tp):
        pl.semaphore_signal(barrier, inc=1, device_id=(to_roll, to_tp), device_id_type=MESH)

    greet(twin, tp)
    for d in range(1, TP):
        greet(roll, lax.rem(tp + d, TP))

    @pl.when(picks)
    def _():
        for d in range(1, ZS):
            greet(at_z(lax.rem(z + d, ZS)), tp)
        for d in range(1, YS):
            greet(at_y(lax.rem(y_hi + d, YS)), tp)

    pl.semaphore_wait(barrier, jnp.where(picks, TP + PICKERS - 1 + YS - 1, TP + PICKERS))

    mine = pl.ds(pl.multiple_of(core * R, R), R)
    theirs = pl.ds(pl.multiple_of((1 - core) * R, R), R)
    p0 = [
        remote(down_hbm.at[theirs], other.at[:, pl.ds(0, ROWS_TP)], p0_send.at[0], p0_recv.at[0], twin, tp),
        remote(up_hbm.at[theirs], other.at[:, pl.ds(ROWS_TP, HD)], p0_send.at[1], p0_recv.at[1], twin, tp),
    ]
    for copy in p0:
        copy.start()
    for copy in loads[:3]:
        copy.wait()
    owner_here = owner[core]
    for copy in p0:
        copy.wait_recv()
    kept = jnp.where(
        owner_here % 2 == core, jnp.concatenate([down[mine, :], up[mine, :]], axis=1), other[...]
    )
    half[...] = kept.reshape(PICKERS, PIECE, WIDTH)

    def to_picker(a):
        return remote(half.at[a], bins_z.at[z], p1_send.at[a], p1_recv.at[z], at_z(a), tp)

    for a in range(PICKERS):
        @pl.when(z != a)
        def _():
            to_picker(a).start()

        @pl.when(z == a)
        def _():
            bins_z[z] = half[a]

    def to_other_y(k):
        return remote(bins_y.at[y_hi], bins_y.at[y_hi], p2_send.at[k], p2_recv.at[y_hi], at_y(k), tp)

    def pick_z():
        for d in range(1, ZS):
            k = lax.rem(z + d, ZS)
            remote(half.at[0], bins_z.at[k], p1_send.at[0], p1_recv.at[k], twin, tp).wait_recv()
        bins_y[y_hi] = bins_z[owner_here // 2 % ZS]
        for d in range(1, YS):
            to_other_y(lax.rem(y_hi + d, YS)).start()

    def to_column(k):
        return remote(now.at[core, z], now.at[core, z], p3_send.at[k], p3_recv.at[z], at_z(k), tp)

    def pick_y():
        for d in range(1, YS):
            k = lax.rem(y_hi + d, YS)
            remote(half.at[0], bins_y.at[k], p2_send.at[0], p2_recv.at[k], twin, tp).wait_recv()
        now[core, z] = bins_y[owner_here // 16]
        for k in range(ZS):
            @pl.when(z != k)
            def _():
                to_column(k).start()

    def hop(c, kind, block, to, src=None, rows=None):
        dst = gathered.at[c, block]
        if rows is not None:
            dst = dst.at[rows]
        return remote(dst if src is None else src, dst, h_send.at[c, kind], h_recv.at[c, kind], roll, to)

    sends = []

    def start(copy):
        copy.start()
        sends.append(copy)

    def landed(c, kind, block, rows=None):
        hop(c, kind, block, across, rows=rows).wait_recv()

    top_rows, low_rows = pl.ds(0, TOK // 2), pl.ds(TOK // 2, TOK // 2)
    far, far_across = pos(x + 2, y), pos(x + 2, 1 - y)
    left_across, right_across = pos(x - 1, 1 - y), pos(x + 1, 1 - y)
    along_y = (0, 1)
    along_x = (2, 3)

    for c in along_x + along_y:
        own = hidden.at[:, pl.ds(c * CHUNK, CHUNK)]
        start(hop(c, 0, tp, across, own))
        start(hop(c, 1, tp, right, own))
        start(hop(c, 2, tp, left, own))

    def pass_on(c):
        landed(c, 1, left)
        start(hop(c, 5, left, right, rows=top_rows))
        if c in along_x:
            start(hop(c, 3, left, across))
        landed(c, 2, right)
        start(hop(c, 6, right, left, rows=low_rows))
        if c in along_x:
            start(hop(c, 4, right, across))

    def spread(c):
        landed(c, 0, across)
        start(hop(c, 3, across, right))
        start(hop(c, 4, across, left))
        pass_on(c)

    def spread_again(c):
        landed(c, 3, left_across)
        start(hop(c, 7, left_across, right, rows=top_rows))
        landed(c, 4, right_across)
        start(hop(c, 8, right_across, left, rows=low_rows))

    def far_across_y(c):
        landed(c, 5, far, top_rows)
        landed(c, 6, far, low_rows)
        start(hop(c, 7, far, across))

    scale = 1.0 / math.sqrt(HD)
    row = lax.broadcasted_iota(jnp.int32, (QPK * GROUP, GROUP * CACHE), 0)
    col = lax.broadcasted_iota(jnp.int32, (QPK * GROUP, GROUP * CACHE), 1)
    same = (row % GROUP) == (col // CACHE)
    col_row = lax.broadcasted_iota(jnp.int32, (1, GROUP * CACHE), 1)

    def block_queries(g, t):
        at = pl.ds(pl.multiple_of(g * GROUP, GROUP), GROUP)
        return jnp.concatenate([queries[t, at, j * HD : (j + 1) * HD] for j in range(QPK)], axis=0)

    def cached(g, _):
        at = pl.ds(pl.multiple_of(g * GROUP, GROUP), GROUP)
        k = kbuf[at].reshape(GROUP * CACHE, HD)
        v = vbuf[at].reshape(GROUP * CACHE, HD)
        length = jnp.zeros((1, GROUP * CACHE), jnp.int32)
        for s in range(GROUP):
            length = jnp.where(col_row // CACHE == s, lens[g * GROUP + s], length)
        live = same & (col_row % CACHE < length)
        for t in range(STEPS):
            q = block_queries(g, t)
            scores = lax.dot_general(q, k, NT, preferred_element_type=jnp.float32) * scale
            scores = jnp.where(live, scores, NEG)
            top = jnp.max(scores, axis=1, keepdims=True)
            w = jnp.exp(scores - top)
            total = jnp.sum(w, axis=1, keepdims=True)
            mixed = jnp.dot(w.astype(jnp.bfloat16), v, preferred_element_type=jnp.float32)
            to = pl.ds(t * QPK * GROUP, QPK * GROUP)
            acc[g, to] = mixed
            top_ref[g, to] = jnp.broadcast_to(top, (QPK * GROUP, HD))
            sum_ref[g, to] = jnp.broadcast_to(total, (QPK * GROUP, HD))
        return 0

    for copy in loads[3:7]:
        copy.wait()
    lax.fori_loop(0, 2, cached, 0)
    for c in along_x:
        pass_on(c)
    lax.fori_loop(2, 4, cached, 0)
    for c in along_y:
        spread(c)
    pl.when(picks)(pick_z)
    for c in along_x:
        far_across_y(c)
    for c in along_y:
        spread_again(c)
    pl.when(picks)(pick_y)

    for copy in loads[7:]:
        copy.wait()
    projected = None
    for c in along_y + along_x:
        if c in along_y:
            landed(c, 5, far, top_rows)
            landed(c, 6, far, low_rows)
            landed(c, 7, far_across, top_rows)
            landed(c, 8, far_across, low_rows)
        else:
            landed(c, 0, across)
            landed(c, 3, left_across)
            landed(c, 4, right_across)
            landed(c, 7, far_across)
        part = jnp.dot(
            gathered[c].reshape(TP * TOK, CHUNK), weights[c * CHUNK : (c + 1) * CHUNK],
            preferred_element_type=jnp.float32,
        )
        projected = part if projected is None else projected + part

    for a in range(PICKERS):
        @pl.when(z != a)
        def _():
            remote(half.at[0], now.at[core, a], p3_send.at[0], p3_recv.at[a], twin, tp).wait_recv()
    p4 = remote(now.at[core], now.at[core], p4_send, p4_recv, twin, tp)
    p4.start()
    remote(now.at[1 - core], now.at[1 - core], p4_send, p4_recv, twin, tp).wait_recv()

    factors = now[...].reshape(2 * R, WIDTH)
    per = CHUNK // ROWS_TP
    mine_hidden = gathered[
        tp // per, :, :, pl.ds(pl.multiple_of(lax.rem(tp, per) * ROWS_TP, ROWS_TP), ROWS_TP)
    ].reshape(TP * TOK, ROWS_TP)
    low_all[tp] = lax.dot_general(
        mine_hidden, factors[:, :ROWS_TP], NT, preferred_element_type=jnp.float32
    ).astype(jnp.bfloat16)

    def all_to(d):
        q = lax.rem(tp + d, TP)
        return remote(low_all.at[tp], low_all.at[tp], g_send.at[q], g_recv.at[tp], roll, q)

    def all_from(d):
        q = lax.rem(tp + d, TP)
        return remote(low_all.at[q], low_all.at[q], g_send.at[q], g_recv.at[q], roll, q)

    for d in range(1, TP):
        all_to(d).start()
    zero = jnp.zeros((R, HD), jnp.bfloat16)
    up_both = jnp.concatenate(
        [
            jnp.concatenate([factors[:R, ROWS_TP:], zero], axis=0),
            jnp.concatenate([zero, factors[R:, ROWS_TP:]], axis=0),
        ],
        axis=1,
    )
    for d in range(1, TP):
        all_from(d).wait_recv()
    low = jnp.sum(low_all[...].astype(jnp.float32), axis=0).astype(jnp.bfloat16)
    projected = projected + jnp.dot(low, up_both, preferred_element_type=jnp.float32)
    fresh = projected.astype(jnp.bfloat16)

    span = GROUP * STEPS
    row2 = lax.broadcasted_iota(jnp.int32, (ROWS, span), 0)
    col2 = lax.broadcasted_iota(jnp.int32, (ROWS, span), 1)
    sample2 = col2 // TOK * (GROUP // 2) + col2 % (GROUP // 2)
    step2 = col2 % TOK // (GROUP // 2)
    live2 = (row2 % GROUP == sample2) & (step2 <= row2 // (QPK * GROUP))
    for g in range(GROUPS):
        q = jnp.concatenate([block_queries(g, t) for t in range(STEPS)], axis=0)
        k = fresh[g * span : (g + 1) * span, :HD]
        v = fresh[g * span : (g + 1) * span, HD:]
        scores = lax.dot_general(q, k, NT, preferred_element_type=jnp.float32) * scale
        scores = jnp.where(live2, scores, NEG)
        old_top = top_ref[g]
        top = jnp.maximum(old_top, jnp.max(scores, axis=1, keepdims=True))
        w = jnp.exp(scores - top[:, :span])
        fade = jnp.exp(old_top - top)
        total = sum_ref[g] * fade + jnp.sum(w, axis=1, keepdims=True)
        mixed = acc[g] * fade + jnp.dot(w.astype(jnp.bfloat16), v, preferred_element_type=jnp.float32)
        done = (mixed / total).astype(jnp.bfloat16)
        for t in range(STEPS):
            for j in range(QPK):
                at = (t * QPK + j) * GROUP
                out[t, g * GROUP : (g + 1) * GROUP, j * HD : (j + 1) * HD] = done[at : at + GROUP]

    for copy in p0 + sends + [p4]:
        copy.wait_send()
    for d in range(1, TP):
        all_to(d).wait_send()
    for a in range(PICKERS):
        @pl.when(z != a)
        def _():
            to_picker(a).wait_send()

    @pl.when(picks)
    def _():
        for d in range(1, YS):
            to_other_y(lax.rem(y_hi + d, YS)).wait_send()
        for d in range(1, ZS):
            to_column(lax.rem(z + d, ZS)).wait_send()


def local(hidden, queries, key_cache, value_cache, cache_len, base_key, base_value, factor_a, factor_b, owner):
    down = jnp.swapaxes(factor_a[0], 1, 2).reshape(2 * R, ROWS_TP)
    up = factor_b[0].reshape(2 * R, HD)
    hbm = pl.BlockSpec(memory_space=pltpu.HBM)
    dma = pltpu.SemaphoreType.DMA
    vmem, bf16, f32 = pltpu.VMEM, jnp.bfloat16, jnp.float32
    return pl.pallas_call(
        kernel,
        out_shape=pltpu.VMEM((STEPS, SAMP, QPK * HD), jnp.bfloat16),
        in_specs=[hbm] * 10,
        out_specs=pl.BlockSpec(memory_space=pltpu.VMEM),
        scratch_shapes=[
            pltpu.SMEM((2,), jnp.int32),
            pltpu.SMEM((SAMP,), jnp.int32),
            vmem((STEPS, SAMP, QPK * HD), bf16),
            vmem((2 * R, ROWS_TP), bf16),
            vmem((2 * R, HD), bf16),
            vmem((NC, TP, TOK, CHUNK), bf16),
            vmem((D, 2 * HD), bf16),
            vmem((SAMP, CACHE, HD), bf16),
            vmem((SAMP, CACHE, HD), bf16),
            vmem((R, WIDTH), bf16),
            vmem((PICKERS, PIECE, WIDTH), bf16),
            vmem((ZS, PIECE, WIDTH), bf16),
            vmem((YS, PIECE, WIDTH), bf16),
            vmem((2, PICKERS, PIECE, WIDTH), bf16),
            vmem((GROUPS, ROWS, HD), f32),
            vmem((GROUPS, ROWS, HD), f32),
            vmem((GROUPS, ROWS, HD), f32),
            vmem((TP, TP * TOK, 2 * R), bf16),
            dma((9 + NC,)),
            dma((2,)), dma((2,)),
            dma((PICKERS,)), dma((ZS,)),
            dma((YS,)), dma((YS,)),
            dma((ZS,)), dma((PICKERS,)),
            dma, dma,
            dma((NC, 9)), dma((NC, 9)),
            dma((TP,)), dma((TP,)),
        ],
        compiler_params=pltpu.CompilerParams(
            collective_id=0, has_side_effects=True, vmem_limit_bytes=60 * 1024 * 1024
        ),
    )(
        owner, cache_len, hidden.reshape(TOK, D), queries, key_cache, value_cache,
        base_key, base_value, down, up,
    )


def solution(mesh):
    placed = (
        P(None, ("roll", "tp"), None),
        P(None, "roll", "tp"),
        P("roll", None, "tp"),
        P("roll", None, "tp"),
        P("roll"),
        P(None, "tp"),
        P(None, "tp"),
        P("roll", None, "tp", None),
        P("roll", None, None, "tp"),
        P(),
    )
    return jax.shard_map(
        local, mesh=mesh, in_specs=placed, out_specs=P(None, "roll", "tp"), check_vma=False
    )
```

time: 59.5 us -> 49.3 us (0.83)
  Pallas kernels: 57.6 us -> 48.5 us
  local copies, waits for them, and re-layouts: 1.67 us -> 0.71 us
    pallas_call x1, Pallas kernels: 57.6 us -> 48.5 us  [local(): pl.pallas_call(kernel, out_shape=pltpu.VMEM((STEPS, SAMP, QPK * HD), jnp....]
    unnamed x1, local copies, waits for them, and re-layouts: 1.67 us -> 0.71 us
where the time goes in v3:
time: 49.3 us; the launch traced here: 49.2 us
  Pallas kernels  48.5 us (98%)
  local copies, waits for them, and re-layouts  0.71 us (1%)
    pallas_call x1, Pallas kernels, local(): pl.pallas_call(kernel, out_shape=pltpu.VMEM((STEPS, SAMP, QPK * HD), jnp....  48.5 us

profile of v3, /device:TPU:1, one launch (start us, length us, event | category | flops | bytes accessed | tf_op | source)
XLA Modules:
  0.0 49.2 jit_solution(9880155964984518894)
XLA Ops:
  0.0 48.5 %shard_map.100 = bf16[4,64,512]{2,1,0:T(8,128)(2,1)S(1)} custom-call(s32[2]{0:T(128)} %owner_hbm.1, s32[64]{0:T(128)} %lens_hbm.1, bf16[32,5120]{1,0:T(8,128)(2,1)} %bitcast.7, bf16[4,64,512]{2,1,0:T(8,128)(2,1)} %queries_hbm.1, bf16[64,32,128]{2,1,0:T(8,128)(2,1)} %keys.1, bf16[64,32,128]{2,1,0:T(8,128)(2,1)} %values.1, bf16[5120,128]{1,0:T(8,128)(2,1)} %base_key.1, ...), custom_call_target="tpu_custom_call" | custom-call | tf_op jit(solution)/shard_map/pallas_call | solution.py:358
  48.5 0.7 %copy.12 = bf16[4,64,512]{2,1,0:T(8,128)(2,1)} copy(bf16[4,64,512]{2,1,0:T(8,128)(2,1)S(1)} %shard_map.100) | data formatting | bytes 524288

commit v4 on v3

--- a/solution.py
+++ b/solution.py
@@ -24,6 +24,7 @@
 ZS = 8
 PICKERS = 4
 YS = 4
+LAST_Y = 2
 GROUP = 16
 GROUPS = SAMP // GROUP
 ROWS = STEPS * QPK * GROUP
@@ -38,7 +39,7 @@
     owner, lens, queries, down, up,
     gathered, weights, kbuf, vbuf, other, half, bins_z, bins_y, now, acc, top_ref, sum_ref, low_all,
     load_sem, p0_send, p0_recv, p1_send, p1_recv, p2_send, p2_recv, p3_send, p3_recv, p4_send, p4_recv,
-    h_send, h_recv, g_send, g_recv,
+    h_send, h_recv, g_send, g_recv, go_z, go_y,
 ):
     roll, tp = lax.axis_index("roll"), lax.axis_index("tp")
     y_hi, z, core = roll // 16, roll // 2 % 8, roll % 2
@@ -75,6 +76,8 @@
         copy.start()
 
     barrier = pltpu.get_barrier_semaphore()
+    tells_y = picks & (y_hi == LAST_Y)
+    asks_y = picks & (y_hi != LAST_Y)
 
     def greet(to_roll, to_tp):
         pl.semaphore_signal(barrier, inc=1, device_id=(to_roll, to_tp), device_id_type=MESH)
@@ -85,12 +88,27 @@
 
     @pl.when(picks)
     def _():
-        for d in range(1, ZS):
-            greet(at_z(lax.rem(z + d, ZS)), tp)
-        for d in range(1, YS):
-            greet(at_y(lax.rem(y_hi + d, YS)), tp)
-
-    pl.semaphore_wait(barrier, jnp.where(picks, TP + PICKERS - 1 + YS - 1, TP + PICKERS))
+        for k in range(PICKERS, ZS):
+            greet(at_z(k), tp)
+
+    @pl.when(asks_y)
+    def _():
+        greet(at_y(LAST_Y), tp)
+
+    pl.semaphore_wait(
+        barrier, TP + jnp.where(picks, 0, PICKERS) + jnp.where(tells_y, YS - 1, 0)
+    )
+
+    @pl.when(z == PICKERS)
+    def _():
+        for k in range(PICKERS):
+            pl.semaphore_signal(go_z, inc=1, device_id=(at_z(k), tp), device_id_type=MESH)
+
+    @pl.when(tells_y)
+    def _():
+        for k in range(YS):
+            if k != LAST_Y:
+                pl.semaphore_signal(go_y, inc=1, device_id=(at_y(k), tp), device_id_type=MESH)
 
     mine = pl.ds(pl.multiple_of(core * R, R), R)
     theirs = pl.ds(pl.multiple_of((1 - core) * R, R), R)
@@ -113,14 +131,21 @@
     def to_picker(a):
         return remote(half.at[a], bins_z.at[z], p1_send.at[a], p1_recv.at[z], at_z(a), tp)
 
-    for a in range(PICKERS):
-        @pl.when(z != a)
-        def _():
+    @pl.when(jnp.logical_not(picks))
+    def _():
+        for a in range(PICKERS):
             to_picker(a).start()
 
-        @pl.when(z == a)
-        def _():
-            bins_z[z] = half[a]
+    def pickers_pieces():
+        pl.semaphore_wait(go_z, 1)
+        for a in range(PICKERS):
+            @pl.when(z != a)
+            def _():
+                to_picker(a).start()
+
+            @pl.when(z == a)
+            def _():
+                bins_z[z] = half[a]
 
     def to_other_y(k):
         return remote(bins_y.at[y_hi], bins_y.at[y_hi], p2_send.at[k], p2_recv.at[y_hi], at_y(k), tp)
@@ -130,8 +155,15 @@
             k = lax.rem(z + d, ZS)
             remote(half.at[0], bins_z.at[k], p1_send.at[0], p1_recv.at[k], twin, tp).wait_recv()
         bins_y[y_hi] = bins_z[owner_here // 2 % ZS]
-        for d in range(1, YS):
-            to_other_y(lax.rem(y_hi + d, YS)).start()
+
+        @pl.when(asks_y)
+        def _():
+            pl.semaphore_wait(go_y, 1)
+
+        for k in range(YS):
+            @pl.when(y_hi != k)
+            def _():
+                to_other_y(k).start()
 
     def to_column(k):
         return remote(now.at[core, z], now.at[core, z], p3_send.at[k], p3_recv.at[z], at_z(k), tp)
@@ -164,8 +196,8 @@
     top_rows, low_rows = pl.ds(0, TOK // 2), pl.ds(TOK // 2, TOK // 2)
     far, far_across = pos(x + 2, y), pos(x + 2, 1 - y)
     left_across, right_across = pos(x - 1, 1 - y), pos(x + 1, 1 - y)
-    along_y = (0, 1)
-    along_x = (2, 3)
+    along_y = (0, 1, 2)
+    along_x = (3,)
 
     for c in along_x + along_y:
         own = hidden.at[:, pl.ds(c * CHUNK, CHUNK)]
@@ -238,6 +270,7 @@
     for c in along_x:
         pass_on(c)
     lax.fori_loop(2, 4, cached, 0)
+    pl.when(picks)(pickers_pieces)
     for c in along_y:
         spread(c)
     pl.when(picks)(pick_z)
@@ -249,23 +282,16 @@
 
     for copy in loads[7:]:
         copy.wait()
-    projected = None
-    for c in along_y + along_x:
-        if c in along_y:
-            landed(c, 5, far, top_rows)
-            landed(c, 6, far, low_rows)
-            landed(c, 7, far_across, top_rows)
-            landed(c, 8, far_across, low_rows)
-        else:
-            landed(c, 0, across)
-            landed(c, 3, left_across)
-            landed(c, 4, right_across)
-            landed(c, 7, far_across)
-        part = jnp.dot(
-            gathered[c].reshape(TP * TOK, CHUNK), weights[c * CHUNK : (c + 1) * CHUNK],
-            preferred_element_type=jnp.float32,
-        )
-        projected = part if projected is None else projected + part
+    for c in along_y:
+        landed(c, 5, far, top_rows)
+        landed(c, 6, far, low_rows)
+        landed(c, 7, far_across, top_rows)
+        landed(c, 8, far_across, low_rows)
+    for c in along_x:
+        landed(c, 0, across)
+        landed(c, 3, left_across)
+        landed(c, 4, right_across)
+        landed(c, 7, far_across)
 
     for a in range(PICKERS):
         @pl.when(z != a)
@@ -273,27 +299,38 @@
             remote(half.at[0], now.at[core, a], p3_send.at[0], p3_recv.at[a], twin, tp).wait_recv()
     p4 = remote(now.at[core], now.at[core], p4_send, p4_recv, twin, tp)
     p4.start()
-    remote(now.at[1 - core], now.at[1 - core], p4_send, p4_recv, twin, tp).wait_recv()
-
-    factors = now[...].reshape(2 * R, WIDTH)
+
     per = CHUNK // ROWS_TP
     mine_hidden = gathered[
         tp // per, :, :, pl.ds(pl.multiple_of(lax.rem(tp, per) * ROWS_TP, ROWS_TP), ROWS_TP)
     ].reshape(TP * TOK, ROWS_TP)
-    low_all[tp] = lax.dot_general(
-        mine_hidden, factors[:, :ROWS_TP], NT, preferred_element_type=jnp.float32
-    ).astype(jnp.bfloat16)
-
-    def all_to(d):
+
+    def multiply(member):
+        down_rows = now[member].reshape(R, WIDTH)[:, :ROWS_TP]
+        low_all[member, tp] = lax.dot_general(
+            down_rows, mine_hidden, NT, preferred_element_type=jnp.float32
+        ).astype(jnp.bfloat16)
+
+    def all_to(member, d):
         q = lax.rem(tp + d, TP)
-        return remote(low_all.at[tp], low_all.at[tp], g_send.at[q], g_recv.at[tp], roll, q)
-
-    def all_from(d):
+        return remote(
+            low_all.at[member, tp], low_all.at[member, tp], g_send.at[member, q], g_recv.at[member, tp], roll, q
+        )
+
+    def all_from(member, d):
         q = lax.rem(tp + d, TP)
-        return remote(low_all.at[q], low_all.at[q], g_send.at[q], g_recv.at[q], roll, q)
-
+        return remote(
+            low_all.at[member, q], low_all.at[member, q], g_send.at[member, q], g_recv.at[member, q], roll, q
+        )
+
+    multiply(core)
     for d in range(1, TP):
-        all_to(d).start()
+        all_to(core, d).start()
+    remote(now.at[1 - core], now.at[1 - core], p4_send, p4_recv, twin, tp).wait_recv()
+    multiply(1 - core)
+    for d in range(1, TP):
+        all_to(1 - core, d).start()
+    factors = now[...].reshape(2 * R, WIDTH)
     zero = jnp.zeros((R, HD), jnp.bfloat16)
     up_both = jnp.concatenate(
         [
@@ -302,10 +339,34 @@
         ],
         axis=1,
     )
-    for d in range(1, TP):
-        all_from(d).wait_recv()
-    low = jnp.sum(low_all[...].astype(jnp.float32), axis=0).astype(jnp.bfloat16)
-    projected = projected + jnp.dot(low, up_both, preferred_element_type=jnp.float32)
+
+    projected = None
+    for c in range(NC):
+        part = jnp.dot(
+            gathered[c].reshape(TP * TOK, CHUNK), weights[c * CHUNK : (c + 1) * CHUNK],
+            preferred_element_type=jnp.float32,
+        )
+        projected = part if projected is None else projected + part
+
+    for copy in p0 + sends + [p4]:
+        copy.wait_send()
+    for a in range(PICKERS):
+        @pl.when(z != a)
+        def _():
+            to_picker(a).wait_send()
+
+    @pl.when(picks)
+    def _():
+        for d in range(1, YS):
+            to_other_y(lax.rem(y_hi + d, YS)).wait_send()
+        for d in range(1, ZS):
+            to_column(lax.rem(z + d, ZS)).wait_send()
+
+    for member in range(2):
+        for d in range(1, TP):
+            all_from(member, d).wait_recv()
+    low = jnp.sum(low_all[...].astype(jnp.float32), axis=1).astype(jnp.bfloat16).reshape(2 * R, TP * TOK)
+    projected = projected + lax.dot_general(low, up_both, TN, preferred_element_type=jnp.float32)
     fresh = projected.astype(jnp.bfloat16)
 
     span = GROUP * STEPS
@@ -332,21 +393,9 @@
                 at = (t * QPK + j) * GROUP
                 out[t, g * GROUP : (g + 1) * GROUP, j * HD : (j + 1) * HD] = done[at : at + GROUP]
 
-    for copy in p0 + sends + [p4]:
-        copy.wait_send()
-    for d in range(1, TP):
-        all_to(d).wait_send()
-    for a in range(PICKERS):
-        @pl.when(z != a)
-        def _():
-            to_picker(a).wait_send()
-
-    @pl.when(picks)
-    def _():
-        for d in range(1, YS):
-            to_other_y(lax.rem(y_hi + d, YS)).wait_send()
-        for d in range(1, ZS):
-            to_column(lax.rem(z + d, ZS)).wait_send()
+    for member in range(2):
+        for d in range(1, TP):
+            all_to(member, d).wait_send()
 
 
 def local(hidden, queries, key_cache, value_cache, cache_len, base_key, base_value, factor_a, factor_b, owner):
@@ -378,7 +427,7 @@
             vmem((GROUPS, ROWS, HD), f32),
             vmem((GROUPS, ROWS, HD), f32),
             vmem((GROUPS, ROWS, HD), f32),
-            vmem((TP, TP * TOK, 2 * R), bf16),
+            vmem((2, TP, R, TP * TOK), bf16),
             dma((9 + NC,)),
             dma((2,)), dma((2,)),
             dma((PICKERS,)), dma((ZS,)),
@@ -386,7 +435,8 @@
             dma((ZS,)), dma((PICKERS,)),
             dma, dma,
             dma((NC, 9)), dma((NC, 9)),
-            dma((TP,)), dma((TP,)),
+            dma((2, TP)), dma((2, TP)),
+            pltpu.SemaphoreType.REGULAR, pltpu.SemaphoreType.REGULAR,
         ],
         compiler_params=pltpu.CompilerParams(
             collective_id=0, has_side_effects=True, vmem_limit_bytes=60 * 1024 * 1024

time: 49.3 us -> 43.7 us (0.89)
  Pallas kernels: 48.5 us -> 42.9 us
    pallas_call x1, Pallas kernels: 48.5 us -> 42.9 us  [local(): pl.pallas_call(kernel, out_shape=pltpu.VMEM((STEPS, SAMP, QPK * HD), jnp....]
where the time goes in v4:
time: 43.7 us; the launch traced here: 43.6 us
  Pallas kernels  42.9 us (98%)
  local copies, waits for them, and re-layouts  0.71 us (2%)
    pallas_call x1, Pallas kernels, local(): pl.pallas_call(kernel, out_shape=pltpu.VMEM((STEPS, SAMP, QPK * HD), jnp....  42.9 us

profile of v4, /device:TPU:1, one launch (start us, length us, event | category | flops | bytes accessed | tf_op | source)
XLA Modules:
  0.0 43.6 jit_solution(7706541560936633019)
XLA Ops:
  0.0 42.9 %shard_map.100 = bf16[4,64,512]{2,1,0:T(8,128)(2,1)S(1)} custom-call(s32[2]{0:T(128)} %owner_hbm.1, s32[64]{0:T(128)} %lens_hbm.1, bf16[32,5120]{1,0:T(8,128)(2,1)} %bitcast.7, bf16[4,64,512]{2,1,0:T(8,128)(2,1)} %queries_hbm.1, bf16[64,32,128]{2,1,0:T(8,128)(2,1)} %keys.1, bf16[64,32,128]{2,1,0:T(8,128)(2,1)} %values.1, bf16[5120,128]{1,0:T(8,128)(2,1)} %base_key.1, ...), custom_call_target="tpu_custom_call" | custom-call | tf_op jit(solution)/shard_map/pallas_call | solution.py:407
  42.9 0.7 %copy.12 = bf16[4,64,512]{2,1,0:T(8,128)(2,1)} copy(bf16[4,64,512]{2,1,0:T(8,128)(2,1)S(1)} %shard_map.100) | data formatting | bytes 524288

commit v5 on v4

--- a/solution.py
+++ b/solution.py
@@ -72,9 +72,6 @@
             + [(hidden.at[:, pl.ds(c * CHUNK, CHUNK)], gathered.at[c, tp]) for c in range(NC)]
         )
     ]
-    for copy in loads:
-        copy.start()
-
     barrier = pltpu.get_barrier_semaphore()
     tells_y = picks & (y_hi == LAST_Y)
     asks_y = picks & (y_hi != LAST_Y)
@@ -95,6 +92,8 @@
     def _():
         greet(at_y(LAST_Y), tp)
 
+    for copy in loads[:3]:
+        copy.start()
     pl.semaphore_wait(
         barrier, TP + jnp.where(picks, 0, PICKERS) + jnp.where(tells_y, YS - 1, 0)
     )
@@ -118,6 +117,8 @@
     ]
     for copy in p0:
         copy.start()
+    for copy in loads[3:]:
+        copy.start()
     for copy in loads[:3]:
         copy.wait()
     owner_here = owner[core]
@@ -133,7 +134,7 @@
 
     @pl.when(jnp.logical_not(picks))
     def _():
-        for a in range(PICKERS):
+        for a in (1, 2, 0, 3):
             to_picker(a).start()
 
     def pickers_pieces():
@@ -270,15 +271,17 @@
     for c in along_x:
         pass_on(c)
     lax.fori_loop(2, 4, cached, 0)
+    spread(along_y[0])
     pl.when(picks)(pickers_pieces)
-    for c in along_y:
+    for c in along_y[1:]:
         spread(c)
     pl.when(picks)(pick_z)
     for c in along_x:
         far_across_y(c)
-    for c in along_y:
+    spread_again(along_y[0])
+    pl.when(picks)(pick_y)
+    for c in along_y[1:]:
         spread_again(c)
-    pl.when(picks)(pick_y)
 
     for copy in loads[7:]:
         copy.wait()

time: 43.7 us -> 43.5 us (level)
  no operation moved by 1% of the time
where the time goes in v5:
time: 43.5 us; the launch traced here: 43.4 us
  Pallas kernels  42.7 us (98%)
  local copies, waits for them, and re-layouts  0.71 us (2%)
    pallas_call x1, Pallas kernels, local(): pl.pallas_call(kernel, out_shape=pltpu.VMEM((STEPS, SAMP, QPK * HD), jnp....  42.7 us

profile of v5, /device:TPU:1, one launch (start us, length us, event | category | flops | bytes accessed | tf_op | source)
XLA Modules:
  0.0 43.4 jit_solution(17250163186694916956)
XLA Ops:
  0.0 42.7 %shard_map.100 = bf16[4,64,512]{2,1,0:T(8,128)(2,1)S(1)} custom-call(s32[2]{0:T(128)} %owner_hbm.1, s32[64]{0:T(128)} %lens_hbm.1, bf16[32,5120]{1,0:T(8,128)(2,1)} %bitcast.7, bf16[4,64,512]{2,1,0:T(8,128)(2,1)} %queries_hbm.1, bf16[64,32,128]{2,1,0:T(8,128)(2,1)} %keys.1, bf16[64,32,128]{2,1,0:T(8,128)(2,1)} %values.1, bf16[5120,128]{1,0:T(8,128)(2,1)} %base_key.1, ...), custom_call_target="tpu_custom_call" | custom-call | tf_op jit(solution)/shard_map/pallas_call | solution.py:410
  42.7 0.7 %copy.12 = bf16[4,64,512]{2,1,0:T(8,128)(2,1)} copy(bf16[4,64,512]{2,1,0:T(8,128)(2,1)S(1)} %shard_map.100) | data formatting | bytes 524288

commit v6 on v5

--- a/solution.py
+++ b/solution.py
@@ -37,7 +37,7 @@
 def kernel(
     owner_hbm, lens_hbm, hidden, queries_hbm, keys, values, base_key, base_value, down_hbm, up_hbm, out,
     owner, lens, queries, down, up,
-    gathered, weights, kbuf, vbuf, other, half, bins_z, bins_y, now, acc, top_ref, sum_ref, low_all,
+    gathered, weights, kbuf, vbuf, other, half, bins_z, bins_y, now, acc, top_ref, sum_ref, low_all, stacked, live2,
     load_sem, p0_send, p0_recv, p1_send, p1_recv, p2_send, p2_recv, p3_send, p3_recv, p4_send, p4_recv,
     h_send, h_recv, g_send, g_recv, go_z, go_y,
 ):
@@ -253,6 +253,7 @@
         live = same & (col_row % CACHE < length)
         for t in range(STEPS):
             q = block_queries(g, t)
+            stacked[g, pl.ds(t * QPK * GROUP, QPK * GROUP)] = q
             scores = lax.dot_general(q, k, NT, preferred_element_type=jnp.float32) * scale
             scores = jnp.where(live, scores, NEG)
             top = jnp.max(scores, axis=1, keepdims=True)
@@ -351,6 +352,13 @@
         )
         projected = part if projected is None else projected + part
 
+    span = GROUP * STEPS
+    row2 = lax.broadcasted_iota(jnp.int32, (ROWS, span), 0)
+    col2 = lax.broadcasted_iota(jnp.int32, (ROWS, span), 1)
+    sample2 = col2 // TOK * (GROUP // 2) + col2 % (GROUP // 2)
+    step2 = col2 % TOK // (GROUP // 2)
+    live2[...] = jnp.where((row2 % GROUP == sample2) & (step2 <= row2 // (QPK * GROUP)), 0.0, NEG)
+
     for copy in p0 + sends + [p4]:
         copy.wait_send()
     for a in range(PICKERS):
@@ -372,18 +380,12 @@
     projected = projected + lax.dot_general(low, up_both, TN, preferred_element_type=jnp.float32)
     fresh = projected.astype(jnp.bfloat16)
 
-    span = GROUP * STEPS
-    row2 = lax.broadcasted_iota(jnp.int32, (ROWS, span), 0)
-    col2 = lax.broadcasted_iota(jnp.int32, (ROWS, span), 1)
-    sample2 = col2 // TOK * (GROUP // 2) + col2 % (GROUP // 2)
-    step2 = col2 % TOK // (GROUP // 2)
-    live2 = (row2 % GROUP == sample2) & (step2 <= row2 // (QPK * GROUP))
     for g in range(GROUPS):
-        q = jnp.concatenate([block_queries(g, t) for t in range(STEPS)], axis=0)
+        q = stacked[g]
         k = fresh[g * span : (g + 1) * span, :HD]
         v = fresh[g * span : (g + 1) * span, HD:]
         scores = lax.dot_general(q, k, NT, preferred_element_type=jnp.float32) * scale
-        scores = jnp.where(live2, scores, NEG)
+        scores = scores + live2[...]
         old_top = top_ref[g]
         top = jnp.maximum(old_top, jnp.max(scores, axis=1, keepdims=True))
         w = jnp.exp(scores - top[:, :span])
@@ -431,6 +433,8 @@
             vmem((GROUPS, ROWS, HD), f32),
             vmem((GROUPS, ROWS, HD), f32),
             vmem((2, TP, R, TP * TOK), bf16),
+            vmem((GROUPS, ROWS, HD), bf16),
+            vmem((ROWS, GROUP * STEPS), f32),
             dma((9 + NC,)),
             dma((2,)), dma((2,)),
             dma((PICKERS,)), dma((ZS,)),

time: 43.5 us -> 43.5 us (level)
  no operation moved by 1% of the time
where the time goes in v6:
time: 43.5 us; the launch traced here: 43.4 us
  Pallas kernels  42.7 us (98%)
  local copies, waits for them, and re-layouts  0.71 us (2%)
    pallas_call x1, Pallas kernels, local(): pl.pallas_call(kernel, out_shape=pltpu.VMEM((STEPS, SAMP, QPK * HD), jnp....  42.7 us

profile of v6, /device:TPU:1, one launch (start us, length us, event | category | flops | bytes accessed | tf_op | source)
XLA Modules:
  0.0 43.4 jit_solution(928157987196577670)
XLA Ops:
  0.0 42.7 %shard_map.100 = bf16[4,64,512]{2,1,0:T(8,128)(2,1)S(1)} custom-call(s32[2]{0:T(128)} %owner_hbm.1, s32[64]{0:T(128)} %lens_hbm.1, bf16[32,5120]{1,0:T(8,128)(2,1)} %bitcast.7, bf16[4,64,512]{2,1,0:T(8,128)(2,1)} %queries_hbm.1, bf16[64,32,128]{2,1,0:T(8,128)(2,1)} %keys.1, bf16[64,32,128]{2,1,0:T(8,128)(2,1)} %values.1, bf16[5120,128]{1,0:T(8,128)(2,1)} %base_key.1, ...), custom_call_target="tpu_custom_call" | custom-call | tf_op jit(solution)/shard_map/pallas_call | solution.py:412
  42.7 0.7 %copy.12 = bf16[4,64,512]{2,1,0:T(8,128)(2,1)} copy(bf16[4,64,512]{2,1,0:T(8,128)(2,1)S(1)} %shard_map.100) | data formatting | bytes 524288
